TPU v7x, 512 devices: a whole 4x8x8 slice. The times are simulated.
512 devices in a mesh: ctx: 64 (over z, y), head: 8 (over x, core).
Axes of the slice: x: 4, y: 8, z: 8, core: 2. Of those that a mesh axis runs over, the one named last changes fastest.
Arguments:
- tokens: bfloat16 [8192, 2048], P('ctx'), may hold values from -6 to 6
- w_query: bfloat16 [2048, 1024], P('ctx', 'head'), may hold values from -0.125 to 0.125
- w_key: bfloat16 [2048, 1024], P('ctx', 'head'), may hold values from -0.125 to 0.125
- w_value: bfloat16 [2048, 2048], P('ctx', 'head'), may hold values from -0.125 to 0.125
- w_output_gate: bfloat16 [2048, 2048], P('ctx', 'head'), may hold values from -0.125 to 0.125
- w_beta: bfloat16 [2048, 16], P('ctx', 'head'), may hold values from -0.125 to 0.125
- w_decay: bfloat16 [2048, 16], P('ctx', 'head'), may hold values from -0.125 to 0.125
- decay_rate: float32 [16], P('head'), may hold values from 0.00024414062 to 0.04
- dt_bias: float32 [16], P('head'), may hold values from -3 to 3
- conv_qk: float32 [4, 2, 1024], P(None, None, 'head'), may hold values from -3 to 3
- conv_value: float32 [4, 2048], P(None, 'head'), may hold values from -3 to 3
- norm_gain: float32 [128], replicated, may hold values from 0.1 to 1.9
- w_out: bfloat16 [2048, 2048], P('head'), may hold values from -0.1875 to 0.1875
- doc_lengths: int32 [32], replicated, may hold values from 1 to 2048, 8192 in all
Outputs:
- mixed: bfloat16 [8192, 2048], P('ctx', 'head')
Inputs may be any that keep to these rules, and one draw needn't show every extreme that they name: `doc_lengths`: the 32 documents lie end to end in this order and cover all 8192 tokens; the longest has exactly 2048 tokens.
All inputs are finite; a program needn't handle non-finite values.
Results may differ from a plain program's by a relative error of at most 0.013.
Values may be sent and summed in bfloat16 or wider, within the bound.
A program may use at most 64 MiB of HBM per device.

v0:
```python
import jax
import jax.numpy as jnp
from jax import lax
from jax.sharding import PartitionSpec as P

HEAD_DIM = 128
SPAN = 64
KERNEL = 4


HIGH = lax.Precision.HIGHEST
EPSILON = 1e-06


def from_behind(value, axis, steps):
    count = lax.axis_size(axis)
    initial, last = (max(0, -steps), min(count, count - steps))
    return lax.ppermute(value, axis, [(source, source + steps) for source in range(initial, last)])


def carried_in(array, axis, combine, identity):
    devices, position = (lax.axis_size(axis), lax.axis_index(axis))
    everything = jax.tree.map(lambda part: lax.all_gather(part, axis), array)
    start = jax.tree.map(
        lambda part, zero: jnp.broadcast_to(jnp.asarray(zero, part.dtype), part.shape),
        array,
        identity,
    )

    def step(k, before):
        reached = k < position
        new = combine(before, jax.tree.map(lambda part: part[k], everything))
        return jax.tree.map(lambda a, b: jnp.where(reached, a, b), new, before)

    return lax.fori_loop(0, devices, step, start)


def segment_of(offsets, positions):
    return jnp.sum((offsets[None, :] <= positions[:, None]).astype(jnp.int32), axis=1)


def short_conv(extended, seg_ext, kernel, length):
    width = kernel.shape[0]
    total = jnp.zeros((length, extended.shape[1]), extended.dtype)
    for tap_index in range(width):
        keep = seg_ext[tap_index : tap_index + length] == seg_ext[width - 1 :]
        total = (
            total
            + jnp.where(keep[:, None], extended[tap_index : tap_index + length], 0.0)
            * kernel[tap_index]
        )
    return jax.nn.silu(total)


def head_inputs(mixed_act, key_heads, beta_logit, decay_logit, decay_rate, dt_bias):
    length = mixed_act.shape[0]
    heads = beta_logit.shape[1]
    inner = key_heads * HEAD_DIM
    queries = mixed_act[:, :inner].reshape(length, key_heads, HEAD_DIM)
    keyed = mixed_act[:, inner : 2 * inner].reshape(length, key_heads, HEAD_DIM)
    values = mixed_act[:, 2 * inner :].reshape(length, heads, HEAD_DIM)
    queries = (
        queries
        * lax.rsqrt(jnp.sum(queries * queries, axis=2, keepdims=True) + EPSILON)
        * HEAD_DIM ** (-0.5)
    )
    keyed = keyed * lax.rsqrt(jnp.sum(keyed * keyed, axis=2, keepdims=True) + EPSILON)
    group = heads // key_heads
    queries = jnp.repeat(queries, group, axis=1)
    keyed = jnp.repeat(keyed, group, axis=1)
    beta = jax.nn.sigmoid(beta_logit)
    decay = -decay_rate * jax.nn.softplus(decay_logit + dt_bias)
    return (queries, keyed, values, beta, decay)


def to_blocks(array):
    length = array.shape[0]
    shaped = array.reshape((length // SPAN, SPAN) + array.shape[1:])
    if array.ndim == 3:
        return shaped.transpose(0, 2, 1, 3)
    return shaped.transpose(0, 2, 1)


def unit_lower_inverse(lower):
    size = lower.shape[-1]
    identity = jnp.eye(size, dtype=lower.dtype)
    inverse = identity - lower
    power = lower
    for level in range(size.bit_length() - 2):
        power = jnp.einsum("hij,hjk->hik", power, power, precision=HIGH)
        inverse = jnp.einsum("hij,hjk->hik", inverse, identity + power, precision=HIGH)
    return inverse


def span_factors(keyed, values, beta, decay, seg, prev_seg):
    size = seg.shape[0]
    gam = jnp.cumsum(decay, axis=1)
    order = jnp.arange(size, dtype=jnp.int32)
    same = (seg[:, None] == seg[None, :]) & (order[:, None] >= order[None, :])
    diff = jnp.where(same[None], gam[:, :, None] - gam[:, None, :], 0.0)
    ratio = jnp.where(same[None], jnp.exp(diff), 0.0)
    lead = jnp.where((seg == prev_seg)[None], jnp.exp(gam), 0.0)
    inner = jnp.einsum("hid,hjd->hij", keyed, keyed, precision=HIGH)
    strict = order[:, None] > order[None, :]
    lower = jnp.where(strict[None], beta[:, :, None] * ratio * inner, 0.0)
    inverse = unit_lower_inverse(lower)
    right = jnp.concatenate([beta[..., None] * values, (beta * lead)[..., None] * keyed], axis=2)
    solved = jnp.einsum("hij,hjd->hid", inverse, right, precision=HIGH)
    return (solved[..., :HEAD_DIM], solved[..., HEAD_DIM:], ratio, lead)


def span_map(keyed, update, writer, ratio, lead):
    tail = ratio[:, -1, :]
    decayed = tail[..., None] * keyed
    identity = jnp.eye(HEAD_DIM, dtype=keyed.dtype)
    transition = lead[:, -1][:, None, None] * identity - jnp.einsum(
        "hjd,hje->hde", writer, decayed, precision=HIGH
    )
    offset_map = jnp.einsum("hjv,hjd->hvd", update, decayed, precision=HIGH)
    return (transition, offset_map)


def span_run(state, queries, keyed, update, writer, ratio, lead):
    fresh = update - jnp.einsum("hcd,hed->hce", writer, state, precision=HIGH)
    scores = jnp.einsum("hid,hjd->hij", queries, keyed, precision=HIGH) * ratio
    carried = jnp.einsum("hcd,hed->hce", queries, state, precision=HIGH)
    result = lead[..., None] * carried + jnp.einsum("hij,hje->hie", scores, fresh, precision=HIGH)
    tail = ratio[:, -1, :]
    new_state = lead[:, -1][:, None, None] * state + jnp.einsum(
        "hje,hjd->hed", fresh, tail[..., None] * keyed, precision=HIGH
    )
    return (new_state, result)


def compose(earlier, later):
    joined_map = jnp.einsum("hab,hbc->hac", earlier[0], later[0], precision=HIGH)
    joined_state = jnp.einsum("hvb,hbc->hvc", earlier[1], later[0], precision=HIGH) + later[1]
    return (joined_map, joined_state)


def gated_norm(result, gate_proj, norm_gain):
    length, heads = (result.shape[0], result.shape[1])
    scaled = (
        result * lax.rsqrt(jnp.mean(result * result, axis=2, keepdims=True) + EPSILON) * norm_gain
    )
    gate = gate_proj.astype(jnp.float32).reshape(length, heads, HEAD_DIM)
    return (scaled * jax.nn.silu(gate)).reshape(length, heads * HEAD_DIM).astype(jnp.bfloat16)


def local(
    tokens,
    w_query,
    w_key,
    w_value,
    w_output_gate,
    w_beta,
    w_decay,
    decay_rate,
    dt_bias,
    conv_qk,
    conv_value,
    norm_gain,
    w_out,
    doc_lengths,
):
    tok_rows = tokens.shape[0]
    key_heads = w_query.shape[1] // HEAD_DIM
    pieces = (
        lax.all_gather(w_query, "ctx", axis=0, tiled=True),
        lax.all_gather(w_key, "ctx", axis=0, tiled=True),
        lax.all_gather(w_value, "ctx", axis=0, tiled=True),
        lax.all_gather(w_output_gate, "ctx", axis=0, tiled=True),
        lax.all_gather(w_beta, "ctx", axis=0, tiled=True),
        lax.all_gather(w_decay, "ctx", axis=0, tiled=True),
    )
    query_f, key_f, value_f, gate_f, beta_logit, decay_logit = tuple(
        (jnp.dot(tokens, piece, preferred_element_type=jnp.float32) for piece in pieces)
    )
    gate_proj = gate_f.astype(jnp.bfloat16)
    joined = jnp.concatenate(
        [query_f.astype(jnp.bfloat16), key_f.astype(jnp.bfloat16), value_f.astype(jnp.bfloat16)],
        axis=1,
    )
    rim = from_behind(joined[tok_rows - (KERNEL - 1) :], "ctx", 1)
    extended = jnp.concatenate([rim, joined], axis=0).astype(jnp.float32)
    offsets = jnp.cumsum(doc_lengths) - doc_lengths
    first = lax.axis_index("ctx") * tok_rows
    positions = first + jnp.arange(-(KERNEL - 1), tok_rows, dtype=jnp.int32)
    seg_ext = segment_of(offsets, positions)
    kernel = jnp.concatenate([conv_qk.reshape(KERNEL, -1), conv_value], axis=1)
    mixed_act = short_conv(extended, seg_ext, kernel, tok_rows)
    queries, keyed, values, beta, decay = head_inputs(
        mixed_act, key_heads, beta_logit, decay_logit, decay_rate, dt_bias
    )
    heads = beta.shape[1]
    token_seg = seg_ext[KERNEL - 1 :].reshape(tok_rows // SPAN, SPAN)
    prev_seg = seg_ext[KERNEL - 2 : KERNEL - 2 + tok_rows : SPAN]
    query_c = to_blocks(queries)
    key_c = to_blocks(keyed)
    identity_map = jnp.broadcast_to(
        jnp.eye(HEAD_DIM, dtype=jnp.float32), (heads, HEAD_DIM, HEAD_DIM)
    )
    empty_state = jnp.zeros((heads, HEAD_DIM, HEAD_DIM), jnp.float32)

    def summarize(carry, items):
        block_map, block_state = carry
        key_b, value_b, beta_b, decay_b, seg_b, prev_b = items
        update, writer, ratio, lead = span_factors(key_b, value_b, beta_b, decay_b, seg_b, prev_b)
        transition, offset_map = span_map(key_b, update, writer, ratio, lead)
        block_map = jnp.einsum("hab,hbc->hac", block_map, transition, precision=HIGH)
        block_state = (
            jnp.einsum("hvb,hbc->hvc", block_state, transition, precision=HIGH) + offset_map
        )
        return ((block_map, block_state), (update, writer, ratio, lead))

    summary, factors = lax.scan(
        summarize,
        (identity_map, empty_state),
        (key_c, to_blocks(values), to_blocks(beta), to_blocks(decay), token_seg, prev_seg),
    )
    prefix = carried_in((summary[0], summary[1]), "ctx", compose, (identity_map, empty_state))

    def advance(state, items):
        query_b, key_b, update, writer, ratio, lead = items
        return span_run(state, query_b, key_b, update, writer, ratio, lead)

    final, outputs = lax.scan(advance, prefix[1], (query_c, key_c) + factors)
    result = outputs.transpose(0, 2, 1, 3).reshape(tok_rows, heads, HEAD_DIM)
    normed = gated_norm(result, gate_proj, norm_gain)
    partial_out = jnp.dot(normed, w_out, preferred_element_type=jnp.float32)
    combined = lax.psum_scatter(partial_out, "head", scatter_dimension=1, tiled=True)
    return combined.astype(jnp.bfloat16)


def solution(mesh):
    return jax.shard_map(
        local,
        mesh=mesh,
        in_specs=(
            P("ctx", None),
            P("ctx", "head"),
            P("ctx", "head"),
            P("ctx", "head"),
            P("ctx", "head"),
            P("ctx", "head"),
            P("ctx", "head"),
            P("head"),
            P("head"),
            P(None, None, "head"),
            P(None, "head"),
            P(),
            P("head", None),
            P(),
        ),
        out_specs=P("ctx", "head"),
        check_vma=False,
    )
```

profile of v0, /device:TPU:1, one launch (start us, length us, event | category | flops | bytes accessed | tf_op | source)
XLA Modules:
  0.0 625.4 jit_solution(16460690747769290667)
XLA Ops:
  8.9 46.6 %all_gather.32 = bf16[2048,128]{1,0:T(8,128)(2,1)S(1)} all-gather(bf16[32,128]{1,0:T(8,128)(2,1)} %param.21), channel_id=1, replica_groups=mesh['ctx'=64,'head'=8] {'ctx'}, dimensions={0}, use_global_device_ids=true | all-gather | bytes 532480 | tf_op jit(solution)/shard_map/all_gather | solution.py:169
  55.5 1.4 convolution_convert_fusion.3
  57.0 37.4 %all_gather.33 = bf16[2048,128]{1,0:T(8,128)(2,1)S(1)} all-gather(bf16[32,128]{1,0:T(8,128)(2,1)} %param.22), channel_id=1, replica_groups=mesh['ctx'=64,'head'=8] {'ctx'}, dimensions={0}, use_global_device_ids=true | all-gather | bytes 532480 | tf_op jit(solution)/shard_map/all_gather | solution.py:170
  94.4 1.4 convolution_convert_fusion.2
  95.9 31.8 %all-gather.2 = bf16[64,32,2]{1,2,0:T(2,128)(2,1)S(1)} all-gather(bf16[1,32,2]{1,2,0:T(2,128)(2,1)} %bitcast.277), channel_id=1, replica_groups=mesh['ctx'=64,'head'=8] {'ctx'}, dimensions={0}, use_global_device_ids=true | all-gather | bytes 8320 | tf_op jit(solution)/shard_map/all_gather | solution.py:174
  129.8 29.2 %all-gather.3 = bf16[64,32,2]{1,2,0:T(2,128)(2,1)S(1)} all-gather(bf16[1,32,2]{1,2,0:T(2,128)(2,1)} %bitcast.278), channel_id=1, replica_groups=mesh['ctx'=64,'head'=8] {'ctx'}, dimensions={0}, use_global_device_ids=true | all-gather | bytes 8320 | tf_op jit(solution)/shard_map/all_gather | solution.py:173
  162.0 1.7 convolution_convert_fusion.1
  163.8 3.4 collective-permute-start
  168.7 13.0 %while.48 = (s32[]{:T(128)}, f32[2,128,128]{1,2,0:T(8,128)S(1)}, f32[2,128,128]{1,2,0:T(8,128)S(1)}, f32[2,2,64,128]{3,2,1,0:T(8,128)S(1)}, f32[2,2,64,128]{3,2,...) while((s32[]{:T(128)}, f32[2,128,128]{1,2,0:T(8,128)S(1)}, ...), condition=%wide.region_5.6_spmd.clone, body=%wide.region_3.5_spmd.clone.sunk | while | flops 252100928 | bytes 3823983 | solution.py:216
  184.0 139.4 %all-gather.13.cloned.1.call-done = f32[128,128,128]{2,1,0:T(8,128)} async-done(((f32[2,128,128]{2,1,0:T(8,128)}), f32[128,128,128]{2,1,0:T(8,128)}) %all-gather.13.cloned.1.call-update) | async-done | bytes 8388624 | tf_op jit(solution)/shard_map/all_gather | solution.py:23
  323.4 100.5 %all-gather.15.cloned.1.call-done = f32[128,128,128]{2,1,0:T(8,128)} async-done(((f32[2,128,128]{2,1,0:T(8,128)}), f32[128,128,128]{2,1,0:T(8,128)}) %all-gather.15.cloned.1.call-update) | async-done | bytes 8388624 | tf_op jit(solution)/shard_map/all_gather | solution.py:23
  423.9 152.1 %while.49 = (s32[]{:T(128)}, f32[2,128,128]{1,2,0:T(8,128)S(1)}, s32[]{:T(128)}, f32[64,2,128,128]{3,2,1,0:T(8,128)}, f32[64,2,128,128]{3,2,1,0:T(8,128)}, /*index=5*/s32[]{:T(128)}, s32[]{:T(128)}) while((s32[]{:T(128)}, f32[2,128,128]{1,2,0:T(8,128)S(1)}, s32[]{:T(128)}, f32[64,2,128,128]{3,2,1,0:T(8,128)}, ...), condition=%wide.region_7.8_spmd.clone, body=%wide.region_6.7_spmd.clone.sunk | while | flops 50462724 | bytes 1443939 | solution.py:35
  425.0 1.3 fusion.247
  427.3 1.3 fusion.247
  439.2 1.3 fusion.247
  441.6 1.3 fusion.247
  444.0 1.3 fusion.247
  451.1 1.3 fusion.247
  455.9 1.3 fusion.247
  460.6 1.3 fusion.247
  463.0 1.3 fusion.247
  465.4 1.3 fusion.247
  474.9 1.3 fusion.247
  477.2 1.3 fusion.247
  484.4 1.3 fusion.247
  491.5 1.3 fusion.247
  493.9 1.3 fusion.247
  496.3 1.3 fusion.247
  576.1 3.8 while.47
  580.6 3.0 fusion.79
  583.6 33.8 %reduce-scatter.2.cloned.1.call-done = f32[128,256]{1,0:T(8,128)} async-done(((f32[128,2048]{1,0:T(8,128)}), f32[128,256]{1,0:T(8,128)}) %reduce-scatter.2.cloned.1.call-update) | async-done | bytes 131088 | tf_op jit(solution)/shard_map/reduce_scatter | solution.py:231
  617.4 1.5 convert_element_type.63
  (397 shorter events, 156.4 us)
Async XLA Ops:
  6.5 574.0 %copy-start = (bf16[256,2048]{1,0:T(8,128)(2,1)S(1)}, bf16[256,2048]{1,0:T(8,128)(2,1)}, u32[]{:S(2)}) copy-start(bf16[256,2048]{1,0:T(8,128)(2,1)} %param.32) | copy-start | bytes 3145732
  6.5 155.5 %all-gather.9.cloned.1.call-start = ((), (), s32[]{:S(2)}) async-start(), calls=%async_computation.1 | async-start | bytes 1064960 | tf_op jit(solution)/shard_map/all_gather | solution.py:171
  7.3 316.1 %all-gather.13.cloned.1.call-start = ((), (), s32[]{:S(2)}) async-start(), calls=%async_computation.4 | async-start | bytes 8519680 | tf_op jit(solution)/shard_map/all_gather | solution.py:23
  163.8 4.2 collective-permute-start
  168.7 15.3 %copy-start.2 = (f32[128]{0:T(128)S(1)}, f32[128]{0:T(128)}, u32[]{:S(2)}) copy-start(f32[128]{0:T(128)} %param.31) | copy-start | bytes 1540
  182.5 241.5 %all-gather.15.cloned.1.call-start = ((), (), s32[]{:S(2)}) async-start(), calls=%async_computation.5 | async-start | bytes 8519680 | tf_op jit(solution)/shard_map/all_gather | solution.py:23
  182.5 398.1 %copy-start.1 = (bf16[128,2048]{1,0:T(8,128)(2,1)S(1)}, bf16[128,2048]{1,0:T(8,128)(2,1)}, u32[]{:S(2)}) copy-start(bf16[128,2048]{1,0:T(8,128)(2,1)} %param.20) | copy-start | bytes 1572868
  183.3 397.0 %all-gather.11.cloned.1.call-start = ((), (), s32[]{:S(2)}) async-start(), calls=%async_computation.2 | async-start | bytes 1064960 | tf_op jit(solution)/shard_map/all_gather | solution.py:172
  183.9 433.5 %reduce-scatter.2.cloned.1.call-start = ((), (), s32[]{:S(2)}) async-start(), calls=%async_computation.3 | async-start | bytes 1179648 | tf_op jit(solution)/shard_map/reduce_scatter | solution.py:231
Sparse Core Ops, SparseCore 0:
  10.4 83.5 all-gather.8
  182.6 140.7 all-gather.12
  326.4 97.4 all-gather.14
  426.8 75.6 all-gather.10
  583.7 33.6 reduce-scatter.1
where the time goes:
time: 629 us; the launch traced here: 625 us
  waiting for transfers between devices  276 us (44%)
  blocking collectives  145 us (23%)
  matrix products  105 us (17%)
  local copies, waits for them, and re-layouts  72.9 us (12%)
  between operations  13.5 us (2%)
  other arithmetic  6.43 us (1%)
    all_gather x2, waiting for transfers between devices, carried_in(): everything = jax.tree.map(lambda part: lax.all_gather(part, axis), array)  240 us
    dot_general x64, matrix products, compose(): jnp.einsum('hvb,hbc->hvc', earlier[1], later[0], precision=HIGH) + later[1]  83.5 us
    dynamic_slice x128, local copies, waits for them, and re-layouts, step(): new = combine(before, jax.tree.map(lambda part: part[k], everything))  64.9 us
    all_gather x1, blocking collectives, local(): lax.all_gather(w_query, 'ctx', axis=0, tiled=True)  46.6 us
    all_gather x1, blocking collectives, local(): lax.all_gather(w_key, 'ctx', axis=0, tiled=True)  37.4 us
    reduce_scatter x1, waiting for transfers between devices, local(): lax.psum_scatter(partial_out, 'head', scatter_dimension=1, tiled=True)  33.8 us
    all_gather x1, blocking collectives, local(): lax.all_gather(w_decay, 'ctx', axis=0, tiled=True)  31.8 us
    all_gather x1, blocking collectives, local(): lax.all_gather(w_beta, 'ctx', axis=0, tiled=True)  29.2 us
  transfers between devices with their start and end apart: 6, of which 4 were waited for; matrix products, arithmetic and copies ran while one was open for 26% of the time, Pallas kernels for 0%

commit v1 on v0

v1 whole, which is shorter than its diff:
```python
import jax
import jax.numpy as jnp
from jax import lax
from jax.experimental import pallas as pl
from jax.experimental.pallas import tpu as pltpu
from jax.sharding import PartitionSpec as P

MESH = pl.DeviceIdType.MESH
HIGH = lax.Precision.HIGHEST
EPSILON = 1e-06
HD = 128
BLOCK = 128
RIM = 16
F32 = jnp.float32
BF16 = jnp.bfloat16
FAR = 1 << 20


def dot(a, b, dims=((1,), (0,)), precision=HIGH):
    return lax.dot_general(a, b, (dims, ((), ())), precision=precision, preferred_element_type=F32)


def iota(shape, dim):
    return lax.broadcasted_iota(jnp.int32, shape, dim)


def unit_lower_inverse(lower):
    size = lower.shape[0]
    row, col = iota(lower.shape, 0), iota(lower.shape, 1)
    inverse = jnp.where(row == col, 1.0, 0.0)
    shift = 0
    while (1 << shift) < size:
        joins = ((row >> (shift + 1)) == (col >> (shift + 1))) & ((row >> shift) != (col >> shift))
        part = jnp.where(joins, lower, 0.0)
        if shift == 0:
            inverse = inverse - part
        else:
            inverse = inverse - dot(dot(inverse, part), inverse)
        shift += 1
    return inverse


def block_state(k, v, beta, g, start):
    row, col = iota((BLOCK, BLOCK), 0), iota((BLOCK, BLOCK), 1)
    lower_tri = row >= col
    gam = dot(jnp.where(lower_tri, 1.0, 0.0), g)
    same = lower_tri & (col >= start)
    ratio = jnp.where(same, jnp.exp(jnp.where(same, gam - gam.T, 0.0)), 0.0)
    lead = jnp.where(start < 0, jnp.exp(gam), 0.0)
    inner = dot(k, k, ((1,), (1,)))
    inverse = unit_lower_inverse(jnp.where(row > col, beta * ratio * inner, 0.0))
    solved = dot(inverse, jnp.concatenate([beta * v, beta * lead * k], axis=1))
    tail = jnp.where(row >= start[BLOCK - 1 :], jnp.exp(gam[BLOCK - 1 :] - gam), 0.0)
    joint = dot(solved, tail * k, ((0,), (0,)))
    transition = jnp.where(row == col, lead[BLOCK - 1 :], 0.0) - joint[HD:]
    return jnp.concatenate([joint[:HD], transition], axis=0), solved, ratio, lead


def block_output(q, k, solved, ratio, lead):
    scores = dot(q, k, ((1,), (1,))) * ratio
    mixed = dot(scores, solved)
    return lead * q - mixed[:, HD:], mixed[:, :HD]


def compose(earlier, later):
    joined = dot(earlier, later[HD:])
    return jnp.concatenate([joined[:HD] + later[:HD], joined[HD:]], axis=0)


def sigmoid(x):
    return 1.0 / (1.0 + jnp.exp(-x))


def kernel(
    tokens, w_query, w_key, w_value, w_gate, w_beta, w_decay, rate, bias, conv_qk, conv_value, gain, w_out, docs,
    out,
    x_all, w_mine, w_other, wo_all, w_stage, piece, pieces, p_mine, p_other, acc, logit,
    z_unit, z_first, z_send, z_in, s_in, n_stage, n_all,
    send_sem, a1_sem, a2_sem, rim_sem, y_sem, p_sem, z_sem, c_sem, wo_sem, par_sem, zf_sem, zi_sem, si_sem, n_sem, own_sem,
):
    ctx, head = lax.axis_index("ctx"), lax.axis_index("head")
    z, y = ctx // 8, ctx % 8
    x, c = head // 2, head % 2
    group, yl, yh = ctx // 4, ctx % 4, (ctx % 8) // 4
    hl = jnp.where(yh == 0, y, 7 - y)
    partner = (ctx, 2 * x + 1 - c)

    def place(g, local):
        g = lax.rem(g + 16, 16)
        return 8 * (g // 2) + jnp.where(g % 2 == 0, local, 7 - local)

    pending = []

    def send(src, dst, recv, device, cond=None):
        copy = pltpu.make_async_remote_copy(
            src_ref=src, dst_ref=dst, send_sem=send_sem.at[len(pending)], recv_sem=recv,
            device_id=device, device_id_type=MESH,
        )
        if cond is None:
            copy.start()
        else:
            pl.when(cond)(copy.start)
        pending.append((copy, cond))

    def arrived(dst, sem):
        pltpu.make_async_copy(dst, dst, sem).wait()

    barrier = pltpu.get_barrier_semaphore()

    def greet(device):
        pl.semaphore_signal(barrier, inc=1, device_id=device, device_id_type=MESH)

    for i in range(1, 8):
        other = 8 * z + lax.rem(y + i, 8)
        greet((other, 2 * x))
        greet((other, 2 * x + 1))
    for i in range(1, 8):
        greet((ctx, lax.rem(head + i, 8)))
    greet((lax.rem(ctx + 8, 64), head))
    greet((lax.rem(ctx + 56, 64), head))
    pl.when((c == 0) & (yh == 0))(lambda: greet((lax.rem(4 * group + 63, 64), 2 * x + 1)))

    @pl.when(c == 1)
    def _():
        for d in range(1, 5):
            greet((place(group - d, hl), head))

    rim_across = (c == 1) & (y == 7)

    for s in range(4):
        for i in range(2):
            p_mine[2 * s + i : 2 * s + i + 1, :] = conv_qk[s, i : i + 1, :]
        for i in range(2):
            p_mine[8 + 4 * i + s : 9 + 4 * i + s, :] = conv_value[s : s + 1, HD * i : HD * i + HD]
    for i in range(2):
        p_mine[16 + 2 * i : 17 + 2 * i, :] = jnp.full((1, HD), rate[i], F32)
        p_mine[17 + 2 * i : 18 + 2 * i, :] = jnp.full((1, HD), bias[i], F32)
    w_stage[0, :, :HD] = w_query[...]
    w_stage[0, :, HD:] = w_key[...]
    for i in range(2):
        w_stage[1 + i, :, :HD] = w_value[:, HD * i : HD * i + HD]
        w_stage[1 + i, :, HD:] = w_gate[:, HD * i : HD * i + HD]
    spot = iota((32, HD), 1) == iota((32, HD), 0) + 32 * (y % 4)
    total = jnp.zeros((16, HD), F32)
    for i, column in enumerate(
        (w_beta[:, 0:1], w_beta[:, 1:2], w_decay[:, 0:1], w_decay[:, 1:2])
    ):
        line = jnp.sum(jnp.where(spot, column.astype(F32), 0.0), axis=0, keepdims=True)
        total = jnp.where(iota((16, HD), 0) == i, line, total)
    piece[...] = total.astype(BF16)

    pl.semaphore_wait(barrier, 23 + 4 * c + 4 * rim_across.astype(jnp.int32))

    mine_rows = pl.ds(pl.multiple_of(32 * y, 32), 32)
    selfs = []
    for sub in range(2):
        local = 2 * c + sub
        for half in range(2):
            to = 8 * z + (local if half == 0 else 7 - local)
            me = to == ctx
            for core in range(2):
                device = (to, 2 * x + core)
                src = w_stage.at[0] if core == 0 else w_stage.at[1 + sub]
                is_self = me & (c == core)
                dst = w_mine.at[z, mine_rows, :]
                send(src, dst, y_sem.at[y], device, ~is_self)
                send(piece, pieces.at[y], p_sem.at[y], device, ~is_self)
                selfs.append((src, dst, is_self))
    for src, dst, is_self in selfs:

        @pl.when(is_self)
        def _(src=src, dst=dst):
            pltpu.make_async_copy(src, dst, y_sem.at[y]).start()
            pltpu.make_async_copy(piece, pieces.at[y], p_sem.at[y]).start()

    quarter = pl.ds(pl.multiple_of(32 * x, 32), 32)
    owner = yl // 2 == c
    for i in range(1, 4):
        to = 4 * group + lax.rem(yl + i, 4)
        rows = pl.ds(pl.multiple_of(RIM + 128 * (yl % 2) + 32 * x, 16), 32)
        send(tokens.at[quarter, :], x_all.at[rows, :], a1_sem.at[yl % 2], (to, head), owner)
    after_two = (c == 0) & (yl == 1)
    after_four = (c == 1) & (yl == 3)
    for i in range(4):
        last = tokens.at[pl.ds(128 - RIM, RIM), :]
        to = jnp.where(after_two, 4 * group + i, lax.rem(4 * group + 4 + i, 64))
        send(last, x_all.at[pl.ds(0, RIM), :], rim_sem, (to, 2 * x + 1 - c), after_two | after_four)
    send(p_mine, p_other, par_sem, partner)
    own_block = []
    for k in range(2):
        is_own = yl == 2 * c + k
        block = x_all.at[pl.ds(RIM + 128 * k, 128), :]
        own_block.append((is_own, pltpu.make_async_copy(tokens, block, own_sem.at[0])))
        pl.when(is_own)(own_block[-1][1].start)
    own_out = pltpu.make_async_copy(
        w_out.at[:, pl.ds(pl.multiple_of(256 * head, 256), 256)],
        wo_all.at[pl.ds(pl.multiple_of(256 * head, 256), 256), :],
        own_sem.at[1],
    )
    own_out.start()

    base = 512 * group + 256 * c
    place_of = iota((256, HD), 0)
    start = jnp.full((256, HD), -FAR, jnp.int32)
    offset = -base
    for i in range(32):
        start = jnp.maximum(start, jnp.where(place_of >= offset, offset, -FAR))
        offset = offset + docs[i]

    for i in range(8):
        arrived(w_mine.at[z, pl.ds(32 * i, 32), :], y_sem.at[i])
        arrived(pieces.at[i], p_sem.at[i])
    for i in range(2):
        joined = sum(pieces[4 * i + j].astype(F32) for j in range(4))
        w_mine[z, 256:272, HD * i : HD * i + HD] = joined.astype(BF16)

    ups, downs = lax.rem(ctx + 8, 64), lax.rem(ctx + 56, 64)
    chunks = (pl.ds(0, 144), pl.ds(144, 128))
    cores = (pl.ds(0, 144), pl.ds(144, 112))

    def onward(bundle, step, way, part):
        ref = w_mine.at[bundle, chunks[part], :]
        send(ref, ref, z_sem.at[way, step - 1, part], (ups if way == 0 else downs, head))

    def across(bundle, part):
        send(w_mine.at[bundle, cores[part], :], w_other.at[bundle, cores[part], :], c_sem.at[bundle, part], partner)

    for part in range(2):
        onward(z, 1, 0, part)
        onward(z, 1, 1, part)
    for part in range(2):
        across(z, part)

    for k in range(2):
        is_remote = yl != 2 * c + k
        rows = pl.ds(pl.multiple_of(RIM + 128 * k + 32 * x, 16), 32)
        pl.when(is_remote)(lambda rows=rows, k=k: arrived(x_all.at[rows, :], a1_sem.at[k]))
        for i in (1, 3, 2):
            device = (ctx, 2 * lax.rem(x + i, 4) + c)
            send(x_all.at[rows, :], x_all.at[rows, :], a2_sem.at[k, i - 1], device, is_remote)
    for i in range(1, 8):
        to = lax.rem(head + i, 8)
        src = w_out.at[:, pl.ds(pl.multiple_of(256 * to, 256), 256)]
        dst = wo_all.at[pl.ds(pl.multiple_of(256 * head, 256), 256), :]
        send(src, dst, wo_sem.at[i - 1], (ctx, to))

    def all_tokens():
        for k in range(2):

            @pl.when(yl != 2 * c + k)
            def _(k=k):
                for i in range(1, 4):
                    rows = pl.ds(pl.multiple_of(RIM + 128 * k + 32 * lax.rem(x + 4 - i, 4), 16), 32)
                    arrived(x_all.at[rows, :], a2_sem.at[k, i - 1])

            pl.when(own_block[k][0])(own_block[k][1].wait)
        arrived(x_all.at[pl.ds(0, RIM), :], rim_sem)

    def multiply(bundle, first):
        rows = x_all[:, pl.ds(pl.multiple_of(256 * bundle, 256), 256)]
        for part in range(2):
            arrived(w_other.at[bundle, cores[part], :], c_sem.at[bundle, part])
        for which, weights in ((c, w_mine), (1 - c, w_other)):
            product = dot(rows, weights[bundle, :256, :], precision=None)
            acc[which] = product if first else acc[which] + product
        small = dot(rows, w_mine[bundle, 256:272, :], ((1,), (1,)), precision=None)
        logit[...] = small if first else logit[...] + small

    for step in range(1, 5):
        below, above = lax.rem(z + 8 - step, 8), lax.rem(z + step, 8)
        for part in range(2):
            for way, bundle in ((0, below), (1, above)):
                if step == 4 and part != way:
                    continue
                arrived(w_mine.at[bundle, chunks[part], :], z_sem.at[way, step - 1, part])
                if step < 3 or (step == 3 and part == way):
                    onward(bundle, step + 1, way, part)
                across(bundle, part)
        if step == 1:
            all_tokens()
            multiply(z, True)
        multiply(below, False)
        if step < 4:
            multiply(above, False)

    arrived(p_other, par_sem)
    settings = jnp.where(hl // 2 == c, p_mine[...], p_other[...])
    second = hl % 2 == 1
    acc[...] = acc[...].astype(BF16).astype(F32)

    def convolved(side, lanes, taps):
        total = acc[side, RIM : RIM + 256, lanes] * taps[3]
        for s in range(3):
            shifted = acc[side, RIM - 3 + s : RIM - 3 + s + 256, lanes]
            total = total + jnp.where(place_of - 3 + s >= start, shifted, 0.0) * taps[s]
        return total * sigmoid(total)

    def pick(low, high):
        return jnp.where(second, settings[high : high + 1], settings[low : low + 1])

    q_act = convolved(0, slice(0, HD), [settings[2 * s : 2 * s + 1] for s in range(4)])
    k_act = convolved(0, slice(HD, 2 * HD), [settings[2 * s + 1 : 2 * s + 2] for s in range(4)])
    v_act = convolved(1, slice(0, HD), [pick(8 + s, 12 + s) for s in range(4)])
    q_act = q_act * (lax.rsqrt(jnp.sum(q_act * q_act, axis=1, keepdims=True) + EPSILON) * HD**-0.5)
    k_act = k_act * lax.rsqrt(jnp.sum(k_act * k_act, axis=1, keepdims=True) + EPSILON)
    logits = logit[RIM:, :]
    beta_logit = jnp.where(second, logits[:, 1:2], logits[:, 0:1])
    decay_logit = jnp.where(second, logits[:, 3:4], logits[:, 2:3])
    beta = jnp.broadcast_to(sigmoid(beta_logit), (256, HD))
    shifted = jnp.broadcast_to(decay_logit, (256, HD)) + pick(17, 19)
    softplus = jnp.maximum(shifted, 0.0) + jnp.log1p(jnp.exp(-jnp.abs(shifted)))
    decay = -pick(16, 18) * softplus

    states, outputs = [], []
    for b in range(2):
        rows = slice(BLOCK * b, BLOCK * b + BLOCK)
        state, solved, ratio, lead = block_state(
            k_act[rows], v_act[rows], beta[rows], decay[rows], start[rows] - BLOCK * b
        )
        states.append(state)
        outputs.append((solved, ratio, lead))
    z_unit[...] = compose(states[0], states[1])
    z_copy = len(pending)
    send(z_unit, z_first, zf_sem, partner, c == 0)

    targets = [(place(group + d, hl), head) for d in range(1, 5)]
    size = [2 * HD, 2 * HD, 2 * HD, HD]

    @pl.when(c == 1)
    def _():
        arrived(z_first, zf_sem)
        z_send[...] = compose(z_first[...], z_unit[...]).astype(BF16)

    for d in range(4):
        part = pl.ds(0, size[d])
        send(z_send.at[part, :], z_in.at[d, part, :], zi_sem.at[d], targets[d], c == 1)

    leads, rests = [], []
    for b in range(2):
        rows = slice(BLOCK * b, BLOCK * b + BLOCK)
        lead_part, rest = block_output(q_act[rows], k_act[rows], *outputs[b])
        if b == 1:
            through = dot(lead_part, states[0], ((1,), (1,)))
            lead_part, rest = through[:, HD:], rest + through[:, :HD]
        leads.append(lead_part)
        rests.append(rest)
    gate = acc[1, RIM:, HD:]
    gate = gate * sigmoid(gate) * gain[...]

    @pl.when(c == 1)
    def _():
        for d in range(4):
            arrived(z_in.at[d, pl.ds(0, size[d]), :], zi_sem.at[d])
        state = z_in[3, :HD].astype(F32)
        for d in (2, 1, 0):
            state = dot(state, z_in[d, HD:].astype(F32)) + z_in[d, :HD].astype(F32)
        s_in[0] = state

    send(s_in.at[0], s_in.at[1], si_sem, partner, c == 1)
    pl.when(c == 0)(lambda: arrived(s_in.at[1], si_sem))

    @pl.when(c == 1)
    def _():
        s_in[1] = dot(s_in[0], z_first[HD:, :]) + z_first[:HD, :]

    before = s_in[1]
    result = dot(jnp.concatenate(leads, axis=0), before, ((1,), (1,))) + jnp.concatenate(rests, axis=0)
    scale = lax.rsqrt(jnp.mean(result * result, axis=1, keepdims=True) + EPSILON)
    n_stage[...] = (result * scale * gate).astype(BF16)

    my_head = 4 * x + hl
    for b in range(2):
        src = n_stage.at[pl.ds(BLOCK * b, BLOCK), :]
        dst = n_all.at[my_head]
        is_self = (yl == 2 * c + b) & (hl % 2 == c)
        device = (4 * group + 2 * c + b, 2 * x + hl % 2)
        send(src, dst, n_sem.at[my_head], device, ~is_self)
        pl.when(is_self)(lambda src=src, dst=dst: pltpu.make_async_copy(src, dst, n_sem.at[my_head]).start())
    for m in range(2):
        which = 4 * x + 2 * m + c
        ref = n_all.at[which]
        arrived(ref, n_sem.at[which])
        for i in (1, 3, 2):
            send(ref, ref, n_sem.at[which], (ctx, 2 * lax.rem(x + i, 4) + c))
        send(ref, ref, n_sem.at[which], partner)
    for i in (1, 3, 2):
        for m in range(2):
            which = 4 * lax.rem(x + i, 4) + 2 * m + c
            ref = n_all.at[which]
            arrived(ref, n_sem.at[which])
            send(ref, ref, n_sem.at[which], partner)
    for i in range(1, 8):
        rows = pl.ds(pl.multiple_of(256 * lax.rem(head + 8 - i, 8), 256), 256)
        arrived(wo_all.at[rows, :], wo_sem.at[i - 1])
    own_out.wait()
    for i in range(8):
        which = 2 * i + 1 - c
        arrived(n_all.at[which], n_sem.at[which])
    total = jnp.zeros((128, 256), F32)
    for i in range(8):
        rows = jnp.concatenate([n_all[2 * i], n_all[2 * i + 1]], axis=1)
        total = total + dot(rows, wo_all[256 * i : 256 * i + 256, :], precision=None)
    out[...] = total.astype(BF16)

    for copy, cond in pending:
        if cond is None:
            copy.wait_send()
        else:
            pl.when(cond)(copy.wait_send)


def local(
    tokens, w_query, w_key, w_value, w_output_gate, w_beta, w_decay, decay_rate, dt_bias, conv_qk, conv_value, norm_gain,
    w_out, doc_lengths,
):
    any_space = pl.BlockSpec(memory_space=pl.ANY)
    vmem = pl.BlockSpec(memory_space=pltpu.VMEM)
    smem = pl.BlockSpec(memory_space=pltpu.SMEM)
    dma = pltpu.SemaphoreType.DMA
    return pl.pallas_call(
        kernel,
        out_shape=jax.ShapeDtypeStruct((128, 256), BF16),
        in_specs=[any_space] + [vmem] * 6 + [smem] * 2 + [vmem] * 3 + [any_space, smem],
        out_specs=vmem,
        scratch_shapes=[
            pltpu.VMEM((RIM + 256, 2048), BF16),
            pltpu.VMEM((8, 272, 256), BF16),
            pltpu.VMEM((8, 256, 256), BF16),
            pltpu.VMEM((2048, 256), BF16),
            pltpu.VMEM((3, 32, 256), BF16),
            pltpu.VMEM((16, HD), BF16),
            pltpu.VMEM((8, 16, HD), BF16),
            pltpu.VMEM((24, HD), F32),
            pltpu.VMEM((24, HD), F32),
            pltpu.VMEM((2, RIM + 256, 256), F32),
            pltpu.VMEM((RIM + 256, 16), F32),
            pltpu.VMEM((2 * HD, HD), F32),
            pltpu.VMEM((2 * HD, HD), F32),
            pltpu.VMEM((2 * HD, HD), BF16),
            pltpu.VMEM((4, 2 * HD, HD), BF16),
            pltpu.VMEM((2, HD, HD), F32),
            pltpu.VMEM((256, HD), BF16),
            pltpu.VMEM((16, 128, HD), BF16),
            dma((110,)),
            dma((2,)),
            dma((2, 3)),
            dma,
            dma((8,)),
            dma((8,)),
            dma((2, 4, 2)),
            dma((8, 2)),
            dma((7,)),
            dma,
            dma,
            dma((4,)),
            dma,
            dma((16,)),
            dma((2,)),
        ],
        compiler_params=pltpu.CompilerParams(
            collective_id=0, has_side_effects=True, vmem_limit_bytes=40 * 2**20
        ),
    )(
        tokens, w_query, w_key, w_value, w_output_gate, w_beta, w_decay, decay_rate, dt_bias, conv_qk, conv_value,
        norm_gain.reshape(1, HD), w_out, doc_lengths,
    )


def solution(mesh):
    return jax.shard_map(
        local,
        mesh=mesh,
        in_specs=(
            P("ctx", None),
            P("ctx", "head"),
            P("ctx", "head"),
            P("ctx", "head"),
            P("ctx", "head"),
            P("ctx", "head"),
            P("ctx", "head"),
            P("head"),
            P("head"),
            P(None, None, "head"),
            P(None, "head"),
            P(),
            P("head", None),
            P(),
        ),
        out_specs=P("ctx", "head"),
        check_vma=False,
    )
```

time: 629 us -> 87.5 us (0.14)
  waiting for transfers between devices: 276 us -> 0 us
  blocking collectives: 145 us -> 0 us
  matrix products: 105 us -> 0 us
  Pallas kernels: 0 us -> 79.1 us
  local copies, waits for them, and re-layouts: 72.9 us -> 7.94 us
  between operations: 13.5 us -> 0.06 us
  other arithmetic: 6.43 us -> 0 us
    all_gather x4 -> x0, waiting for transfers between devices: 240 us -> none  [the longest x2 240 us: carried_in(): everything = jax.tree.map(lambda part: lax.all_gather(part, axis), array)]
    all_gather x4 -> x0, blocking collectives: 145 us -> none  [the longest x1 46.6 us: local(): lax.all_gather(w_query, 'ctx', axis=0, tiled=True)]
    dot_general x112 -> x0, matrix products: 105 us -> none  [the longest x64 83.5 us: compose(): jnp.einsum('hvb,hbc->hvc', earlier[1], later[0], precision=HIGH) + later[1]]
    pallas_call x0 -> x1, Pallas kernels: none -> 79.1 us  [local(): pl.pallas_call(kernel, out_shape=jax.ShapeDtypeStruct((128, 256), BF16),...]
    dynamic_slice x130 -> x0, local copies, waits for them, and re-layouts: 66.2 us -> none  [the longest x128 64.9 us: step(): new = combine(before, jax.tree.map(lambda part: part[k], everything))]
    reduce_scatter x1 -> x0, waiting for transfers between devices: 33.8 us -> none  [local(): lax.psum_scatter(partial_out, 'head', scatter_dimension=1, tiled=True)]
    unnamed x9 -> x29, local copies, waits for them, and re-layouts: 0.93 us -> 7.94 us
  transfers between devices with their start and end apart: 6 -> 0, of which waited for: 4 -> 0; matrix products, arithmetic and copies ran while one was open for 26% -> 0% of each run, Pallas kernels for 0% -> 0%
where the time goes in v1:
time: 87.5 us; the launch traced here: 87.1 us
  Pallas kernels  79.1 us (90%)
  local copies, waits for them, and re-layouts  7.94 us (9%)
    pallas_call x1, Pallas kernels, local(): pl.pallas_call(kernel, out_shape=jax.ShapeDtypeStruct((128, 256), BF16),...  79.1 us
    unnamed x29, local copies, waits for them, and re-layouts  7.94 us

profile of v1, /device:TPU:1, one launch (start us, length us, event | category | flops | bytes accessed | tf_op | source)
XLA Modules:
  0.0 87.1 jit_solution(9747886674722655277)
XLA Ops:
  0.0 0.0 copy-start.12
  0.0 0.0 copy-start.2
  0.0 0.7 copy-done.12
  0.7 0.1 copy.15.w_beta
  0.8 0.0 copy-start.8
  0.8 0.0 copy-start.9
  0.8 0.0 copy-start.10
  0.8 0.0 copy-start.11
  0.8 0.8 copy.16.w_decay
  1.6 0.0 copy-done.2
  1.6 0.0 copy-done.8
  1.6 0.0 copy-done.9
  1.6 0.0 copy-done.10
  1.6 0.0 copy-done.11
  1.6 0.0 copy-start
  1.6 1.2 %copy-done = bf16[256,2048]{1,0:T(8,128)(2,1)S(1)} copy-done((bf16[256,2048]{1,0:T(8,128)(2,1)S(1)}, bf16[256,2048]{1,0:T(8,128)(2,1)}, u32[]{:S(2)}) %copy-start) | copy-done | bytes 1048600
  2.8 0.0 copy-start.1
  2.8 1.0 %copy-done.1 = bf16[128,2048]{1,0:T(8,128)(2,1)S(1)} copy-done((bf16[128,2048]{1,0:T(8,128)(2,1)S(1)}, bf16[128,2048]{1,0:T(8,128)(2,1)}, u32[]{:S(2)}) %copy-start.1) | copy-done | bytes 524312
  3.9 0.0 copy-start.3
  3.9 0.7 copy-done.3
  4.6 0.0 copy-start.4
  4.6 0.7 copy-done.4
  5.3 0.0 copy-start.5
  5.3 0.7 copy-done.5
  6.0 0.0 copy-start.6
  6.0 0.7 copy-done.6
  6.7 0.0 copy-start.7
  6.7 0.7 copy-done.7
  7.4 79.1 %shard_map.136 = bf16[128,256]{1,0:T(8,128)(2,1)S(1)} custom-call(bf16[128,2048]{1,0:T(8,128)(2,1)S(1)} %copy-done.1, bf16[32,128]{1,0:T(8,128)(2,1)S(1)} %copy-done.4, bf16[32,128]{1,0:T(8,128)(2,1)S(1)} %copy-done.5, bf16[32,256]{1,0:T(8,128)(2,1)S(1)} %copy-done.2, bf16[32,256]{1,0:T(8,128)(2,1)S(1)} %copy-done.3, bf16[32,2]{1,0:T(8,128)(2,1)S(1)} %copy.15.w_beta, ...), custom_call_target="tpu_custom_call" | custom-call | tf_op jit(solution)/shard_map/pallas_call | solution.py:420
  86.4 0.6 copy.18
Async XLA Ops:
  0.0 0.7 copy-start.12
  0.0 1.6 %copy-start.2 = (bf16[32,256]{1,0:T(8,128)(2,1)S(1)}, bf16[32,256]{1,0:T(8,128)(2,1)}, u32[]{:S(2)}) copy-start(bf16[32,256]{1,0:T(8,128)(2,1)} %w_value.1) | copy-start | bytes 49156
  0.8 0.8 copy-start.8
  0.8 0.8 copy-start.9
  0.8 0.8 copy-start.10
  0.8 0.8 copy-start.11
  1.6 1.2 %copy-start = (bf16[256,2048]{1,0:T(8,128)(2,1)S(1)}, bf16[256,2048]{1,0:T(8,128)(2,1)}, u32[]{:S(2)}) copy-start(bf16[256,2048]{1,0:T(8,128)(2,1)} %w_out.1) | copy-start | bytes 3145732
  2.8 1.0 %copy-start.1 = (bf16[128,2048]{1,0:T(8,128)(2,1)S(1)}, bf16[128,2048]{1,0:T(8,128)(2,1)}, u32[]{:S(2)}) copy-start(bf16[128,2048]{1,0:T(8,128)(2,1)} %tokens.1) | copy-start | bytes 1572868
  3.9 0.7 copy-start.3
  4.6 0.7 copy-start.4
  5.3 0.7 copy-start.5
  6.0 0.7 copy-start.6
  6.7 0.7 copy-start.7

commit v2 on v1

--- a/solution.py
+++ b/solution.py
@@ -72,11 +72,14 @@
 
 
 def kernel(
-    tokens, w_query, w_key, w_value, w_gate, w_beta, w_decay, rate, bias, conv_qk, conv_value, gain, w_out, docs,
+    tokens, w_query, w_key, w_value, w_gate, w_beta, w_decay, rate_in, bias_in, conv_qk_in, conv_value_in, gain_in, w_out,
+    docs_in,
     out,
+    beta_w, rate, bias, conv_qk, conv_value, gain, docs,
     x_all, w_mine, w_other, wo_all, w_stage, piece, pieces, p_mine, p_other, acc, logit,
     z_unit, z_first, z_send, z_in, s_in, n_stage, n_all,
     send_sem, a1_sem, a2_sem, rim_sem, y_sem, p_sem, z_sem, c_sem, wo_sem, par_sem, zf_sem, zi_sem, si_sem, n_sem, own_sem,
+    in_sem,
 ):
     ctx, head = lax.axis_index("ctx"), lax.axis_index("head")
     z, y = ctx // 8, ctx % 8
@@ -105,6 +108,30 @@
     def arrived(dst, sem):
         pltpu.make_async_copy(dst, dst, sem).wait()
 
+    inputs = [
+        pltpu.make_async_copy(src, dst, in_sem.at[i])
+        for i, (src, dst) in enumerate(
+            [
+                (w_query, w_stage.at[0, :, :HD]),
+                (w_key, w_stage.at[0, :, HD:]),
+                (w_value.at[:, :HD], w_stage.at[1, :, :HD]),
+                (w_value.at[:, HD:], w_stage.at[2, :, :HD]),
+                (w_gate.at[:, :HD], w_stage.at[1, :, HD:]),
+                (w_gate.at[:, HD:], w_stage.at[2, :, HD:]),
+                (w_beta, beta_w.at[0]),
+                (w_decay, beta_w.at[1]),
+                (rate_in, rate),
+                (bias_in, bias),
+                (conv_qk_in, conv_qk),
+                (conv_value_in, conv_value),
+                (gain_in, gain),
+                (docs_in, docs),
+            ]
+        )
+    ]
+    for copy in inputs:
+        copy.start()
+
     barrier = pltpu.get_barrier_semaphore()
 
     def greet(device):
@@ -127,6 +154,8 @@
 
     rim_across = (c == 1) & (y == 7)
 
+    for copy in inputs:
+        copy.wait()
     for s in range(4):
         for i in range(2):
             p_mine[2 * s + i : 2 * s + i + 1, :] = conv_qk[s, i : i + 1, :]
@@ -135,19 +164,13 @@
     for i in range(2):
         p_mine[16 + 2 * i : 17 + 2 * i, :] = jnp.full((1, HD), rate[i], F32)
         p_mine[17 + 2 * i : 18 + 2 * i, :] = jnp.full((1, HD), bias[i], F32)
-    w_stage[0, :, :HD] = w_query[...]
-    w_stage[0, :, HD:] = w_key[...]
-    for i in range(2):
-        w_stage[1 + i, :, :HD] = w_value[:, HD * i : HD * i + HD]
-        w_stage[1 + i, :, HD:] = w_gate[:, HD * i : HD * i + HD]
-    spot = iota((32, HD), 1) == iota((32, HD), 0) + 32 * (y % 4)
-    total = jnp.zeros((16, HD), F32)
-    for i, column in enumerate(
-        (w_beta[:, 0:1], w_beta[:, 1:2], w_decay[:, 0:1], w_decay[:, 1:2])
-    ):
-        line = jnp.sum(jnp.where(spot, column.astype(F32), 0.0), axis=0, keepdims=True)
-        total = jnp.where(iota((16, HD), 0) == i, line, total)
-    piece[...] = total.astype(BF16)
+    piece[...] = jnp.zeros((16, HD), BF16)
+    for q in range(4):
+
+        @pl.when(y % 4 == q)
+        def _(q=q):
+            piece[0:2, 32 * q : 32 * q + 32] = beta_w[0]
+            piece[2:4, 32 * q : 32 * q + 32] = beta_w[1]
 
     pl.semaphore_wait(barrier, 23 + 4 * c + 4 * rim_across.astype(jnp.int32))
 
@@ -413,16 +436,21 @@
     tokens, w_query, w_key, w_value, w_output_gate, w_beta, w_decay, decay_rate, dt_bias, conv_qk, conv_value, norm_gain,
     w_out, doc_lengths,
 ):
-    any_space = pl.BlockSpec(memory_space=pl.ANY)
     vmem = pl.BlockSpec(memory_space=pltpu.VMEM)
-    smem = pl.BlockSpec(memory_space=pltpu.SMEM)
     dma = pltpu.SemaphoreType.DMA
     return pl.pallas_call(
         kernel,
         out_shape=jax.ShapeDtypeStruct((128, 256), BF16),
-        in_specs=[any_space] + [vmem] * 6 + [smem] * 2 + [vmem] * 3 + [any_space, smem],
+        in_specs=[pl.BlockSpec(memory_space=pltpu.HBM)] * 14,
         out_specs=vmem,
         scratch_shapes=[
+            pltpu.VMEM((2, 2, 32), BF16),
+            pltpu.SMEM((2,), F32),
+            pltpu.SMEM((2,), F32),
+            pltpu.VMEM((4, 2, HD), F32),
+            pltpu.VMEM((4, 256), F32),
+            pltpu.VMEM((1, HD), F32),
+            pltpu.SMEM((32,), jnp.int32),
             pltpu.VMEM((RIM + 256, 2048), BF16),
             pltpu.VMEM((8, 272, 256), BF16),
             pltpu.VMEM((8, 256, 256), BF16),
@@ -456,12 +484,13 @@
             dma,
             dma((16,)),
             dma((2,)),
+            dma((14,)),
         ],
         compiler_params=pltpu.CompilerParams(
-            collective_id=0, has_side_effects=True, vmem_limit_bytes=40 * 2**20
+            collective_id=0, has_side_effects=True, vmem_limit_bytes=60 * 2**20
         ),
     )(
-        tokens, w_query, w_key, w_value, w_output_gate, w_beta, w_decay, decay_rate, dt_bias, conv_qk, conv_value,
+        tokens, w_query, w_key, w_value, w_output_gate, w_beta.T, w_decay.T, decay_rate, dt_bias, conv_qk, conv_value,
         norm_gain.reshape(1, HD), w_out, doc_lengths,
     )
 

time: 87.5 us -> 80.9 us (0.925)
  local copies, waits for them, and re-layouts: 7.94 us -> 1.47 us
    unnamed x29 -> x1, local copies, waits for them, and re-layouts: 7.94 us -> 1.47 us
where the time goes in v2:
time: 80.9 us; the launch traced here: 80.7 us
  Pallas kernels  79.2 us (98%)
  local copies, waits for them, and re-layouts  1.47 us (2%)
    pallas_call x1, Pallas kernels, local(): pl.pallas_call(kernel, out_shape=jax.ShapeDtypeStruct((128, 256), BF16),...  79.2 us

profile of v2, /device:TPU:1, one launch (start us, length us, event | category | flops | bytes accessed | tf_op | source)
XLA Modules:
  0.0 80.7 jit_solution(8464655917693053858)
XLA Ops:
  0.0 79.2 %shard_map.136 = bf16[128,256]{1,0:T(8,128)(2,1)} custom-call(bf16[128,2048]{1,0:T(8,128)(2,1)} %tokens.1, bf16[32,128]{1,0:T(8,128)(2,1)} %w_query.1, bf16[32,128]{1,0:T(8,128)(2,1)} %w_key.1, bf16[32,256]{1,0:T(8,128)(2,1)} %w_value.1, bf16[32,256]{1,0:T(8,128)(2,1)} %w_gate.1, bf16[2,32]{1,0:T(2,128)(2,1)} %bitcast.3, bf16[2,32]{1,0:T(2,128)(2,1)} %bitcast.4, ...), custom_call_target="tpu_custom_call" | custom-call | tf_op jit(solution)/shard_map/pallas_call | solution.py:441
  79.2 1.5 %copy.16 = bf16[128,256]{1,0:T(8,128)(2,1)} copy(bf16[128,256]{1,0:T(8,128)(2,1)} %shard_map.136) | data formatting | bytes 131072

commit v3 on v2

--- a/solution.py
+++ b/solution.py
@@ -6,7 +6,6 @@
 from jax.sharding import PartitionSpec as P
 
 MESH = pl.DeviceIdType.MESH
-HIGH = lax.Precision.HIGHEST
 EPSILON = 1e-06
 HD = 128
 BLOCK = 128
@@ -16,55 +15,85 @@
 FAR = 1 << 20
 
 
-def dot(a, b, dims=((1,), (0,)), precision=HIGH):
-    return lax.dot_general(a, b, (dims, ((), ())), precision=precision, preferred_element_type=F32)
+def dot(a, b, dims=((1,), (0,))):
+    return lax.dot_general(a, b, (dims, ((), ())), preferred_element_type=F32)
+
+
+def halves(a):
+    high = a.astype(BF16)
+    return high, (a - high.astype(F32)).astype(BF16)
+
+
+def dot3(a, b):
+    width = b.shape[1]
+    (a_high, a_low), (b_high, b_low) = halves(a), halves(b)
+    left = jnp.concatenate([a_high, a_low], axis=1)
+    right = jnp.concatenate(
+        [jnp.concatenate([b_high, b_low], axis=1), jnp.concatenate([b_high, jnp.zeros_like(b_low)], axis=1)], axis=0
+    )
+    both = dot(left, right)
+    return both[:, :width] + both[:, width:]
+
+
+def dot2(a, b):
+    width = b.shape[1]
+    both = dot(a, jnp.concatenate(halves(b), axis=1))
+    return both[:, :width] + both[:, width:]
 
 
 def iota(shape, dim):
     return lax.broadcasted_iota(jnp.int32, shape, dim)
 
 
-def unit_lower_inverse(lower):
-    size = lower.shape[0]
-    row, col = iota(lower.shape, 0), iota(lower.shape, 1)
-    inverse = jnp.where(row == col, 1.0, 0.0)
+def each(function, *lists):
+    return [function(*items) for items in zip(*lists)]
+
+
+def unit_lower_inverses(lowers):
+    size = lowers[0].shape[0]
+    row, col = iota((size, size), 0), iota((size, size), 1)
+    inverses = each(lambda lower: jnp.where(row == col, 1.0, 0.0), lowers)
     shift = 0
     while (1 << shift) < size:
         joins = ((row >> (shift + 1)) == (col >> (shift + 1))) & ((row >> shift) != (col >> shift))
-        part = jnp.where(joins, lower, 0.0)
-        if shift == 0:
-            inverse = inverse - part
-        else:
-            inverse = inverse - dot(dot(inverse, part), inverse)
+        parts = each(lambda lower: jnp.where(joins, lower, 0.0), lowers)
+        if shift > 0:
+            parts = each(dot3, each(dot3, inverses, parts), inverses)
+        inverses = each(lambda inverse, part: inverse - part, inverses, parts)
         shift += 1
-    return inverse
-
-
-def block_state(k, v, beta, g, start):
+    return inverses
+
+
+def block_states(k, v, beta, g, start):
     row, col = iota((BLOCK, BLOCK), 0), iota((BLOCK, BLOCK), 1)
     lower_tri = row >= col
-    gam = dot(jnp.where(lower_tri, 1.0, 0.0), g)
-    same = lower_tri & (col >= start)
-    ratio = jnp.where(same, jnp.exp(jnp.where(same, gam - gam.T, 0.0)), 0.0)
-    lead = jnp.where(start < 0, jnp.exp(gam), 0.0)
-    inner = dot(k, k, ((1,), (1,)))
-    inverse = unit_lower_inverse(jnp.where(row > col, beta * ratio * inner, 0.0))
-    solved = dot(inverse, jnp.concatenate([beta * v, beta * lead * k], axis=1))
-    tail = jnp.where(row >= start[BLOCK - 1 :], jnp.exp(gam[BLOCK - 1 :] - gam), 0.0)
-    joint = dot(solved, tail * k, ((0,), (0,)))
-    transition = jnp.where(row == col, lead[BLOCK - 1 :], 0.0) - joint[HD:]
-    return jnp.concatenate([joint[:HD], transition], axis=0), solved, ratio, lead
-
-
-def block_output(q, k, solved, ratio, lead):
-    scores = dot(q, k, ((1,), (1,))) * ratio
-    mixed = dot(scores, solved)
-    return lead * q - mixed[:, HD:], mixed[:, :HD]
+    ones = jnp.where(lower_tri, 1.0, 0.0).astype(BF16)
+    gam = each(lambda g: dot2(ones, g), g)
+    inner = each(lambda k: dot3(k, k.T), k)
+    ratio, lead, lower = [], [], []
+    for b in range(len(k)):
+        same = lower_tri & (col >= start[b])
+        ratio.append(jnp.where(same, jnp.exp(jnp.where(same, gam[b] - gam[b].T, 0.0)), 0.0))
+        lead.append(jnp.where(start[b] < 0, jnp.exp(gam[b]), 0.0))
+        lower.append(jnp.where(row > col, beta[b] * ratio[b] * inner[b], 0.0))
+    rights, lasts = [], []
+    for b in range(len(k)):
+        rights.append(jnp.concatenate([beta[b] * v[b], beta[b] * lead[b] * k[b]], axis=1))
+        tail = jnp.where(row >= start[b][BLOCK - 1 :], jnp.exp(gam[b][BLOCK - 1 :] - gam[b]), 0.0)
+        lasts.append((tail * k[b]).T)
+    inverses = unit_lower_inverses(lower)
+    solved = each(dot3, inverses, rights)
+    joint = each(dot3, lasts, solved)
+    states = []
+    for b in range(len(k)):
+        transition = jnp.where(row == col, lead[b][BLOCK - 1 :], 0.0) - joint[b][:, HD:]
+        states.append(jnp.concatenate([joint[b][:, :HD], transition], axis=1))
+    return states, solved, ratio, lead
 
 
 def compose(earlier, later):
-    joined = dot(earlier, later[HD:])
-    return jnp.concatenate([joined[:HD] + later[:HD], joined[HD:]], axis=0)
+    joined = dot3(later[:, HD:], earlier)
+    return jnp.concatenate([joined[:, :HD] + later[:, :HD], joined[:, HD:]], axis=1)
 
 
 def sigmoid(x):
@@ -105,8 +134,36 @@
             pl.when(cond)(copy.start)
         pending.append((copy, cond))
 
+    def sent(copy, cond):
+        if cond is None:
+            copy.wait_send()
+        else:
+            pl.when(cond)(copy.wait_send)
+
     def arrived(dst, sem):
         pltpu.make_async_copy(dst, dst, sem).wait()
+
+    barrier = pltpu.get_barrier_semaphore()
+
+    def greet(device):
+        pl.semaphore_signal(barrier, inc=1, device_id=device, device_id_type=MESH)
+
+    for i in range(1, 8):
+        other = 8 * z + lax.rem(y + i, 8)
+        greet((other, 2 * x))
+        greet((other, 2 * x + 1))
+    for i in range(1, 8):
+        greet((ctx, lax.rem(head + i, 8)))
+    greet((lax.rem(ctx + 8, 64), head))
+    greet((lax.rem(ctx + 56, 64), head))
+    pl.when((c == 0) & (yh == 0))(lambda: greet((lax.rem(4 * group + 63, 64), 2 * x + 1)))
+
+    @pl.when(c == 1)
+    def _():
+        for d in range(1, 5):
+            greet((place(group - d, hl), head))
+
+    rim_across = (c == 1) & (y == 7)
 
     inputs = [
         pltpu.make_async_copy(src, dst, in_sem.at[i])
@@ -132,28 +189,6 @@
     for copy in inputs:
         copy.start()
 
-    barrier = pltpu.get_barrier_semaphore()
-
-    def greet(device):
-        pl.semaphore_signal(barrier, inc=1, device_id=device, device_id_type=MESH)
-
-    for i in range(1, 8):
-        other = 8 * z + lax.rem(y + i, 8)
-        greet((other, 2 * x))
-        greet((other, 2 * x + 1))
-    for i in range(1, 8):
-        greet((ctx, lax.rem(head + i, 8)))
-    greet((lax.rem(ctx + 8, 64), head))
-    greet((lax.rem(ctx + 56, 64), head))
-    pl.when((c == 0) & (yh == 0))(lambda: greet((lax.rem(4 * group + 63, 64), 2 * x + 1)))
-
-    @pl.when(c == 1)
-    def _():
-        for d in range(1, 5):
-            greet((place(group - d, hl), head))
-
-    rim_across = (c == 1) & (y == 7)
-
     for copy in inputs:
         copy.wait()
     for s in range(4):
@@ -196,18 +231,20 @@
             pltpu.make_async_copy(src, dst, y_sem.at[y]).start()
             pltpu.make_async_copy(piece, pieces.at[y], p_sem.at[y]).start()
 
-    quarter = pl.ds(pl.multiple_of(32 * x, 32), 32)
-    owner = yl // 2 == c
-    for i in range(1, 4):
-        to = 4 * group + lax.rem(yl + i, 4)
-        rows = pl.ds(pl.multiple_of(RIM + 128 * (yl % 2) + 32 * x, 16), 32)
-        send(tokens.at[quarter, :], x_all.at[rows, :], a1_sem.at[yl % 2], (to, head), owner)
-    after_two = (c == 0) & (yl == 1)
-    after_four = (c == 1) & (yl == 3)
-    for i in range(4):
-        last = tokens.at[pl.ds(128 - RIM, RIM), :]
-        to = jnp.where(after_two, 4 * group + i, lax.rem(4 * group + 4 + i, 64))
-        send(last, x_all.at[pl.ds(0, RIM), :], rim_sem, (to, 2 * x + 1 - c), after_two | after_four)
+    def tokens_out():
+        quarter = pl.ds(pl.multiple_of(32 * x, 32), 32)
+        owner = yl // 2 == c
+        for i in range(1, 4):
+            to = 4 * group + lax.rem(yl + i, 4)
+            rows = pl.ds(pl.multiple_of(RIM + 128 * (yl % 2) + 32 * x, 16), 32)
+            send(tokens.at[quarter, :], x_all.at[rows, :], a1_sem.at[yl % 2], (to, head), owner)
+        after_two = (c == 0) & (yl == 1)
+        after_four = (c == 1) & (yl == 3)
+        for i in range(4):
+            last = tokens.at[pl.ds(128 - RIM, RIM), :]
+            to = jnp.where(after_two, 4 * group + i, lax.rem(4 * group + 4 + i, 64))
+            send(last, x_all.at[pl.ds(0, RIM), :], rim_sem, (to, 2 * x + 1 - c), after_two | after_four)
+
     send(p_mine, p_other, par_sem, partner)
     own_block = []
     for k in range(2):
@@ -238,7 +275,7 @@
         w_mine[z, 256:272, HD * i : HD * i + HD] = joined.astype(BF16)
 
     ups, downs = lax.rem(ctx + 8, 64), lax.rem(ctx + 56, 64)
-    chunks = (pl.ds(0, 144), pl.ds(144, 128))
+    chunks = [pl.ds(at, size) for at, size in ((0, 80), (80, 64), (144, 64), (208, 64))]
     cores = (pl.ds(0, 144), pl.ds(144, 112))
 
     def onward(bundle, step, way, part):
@@ -248,24 +285,26 @@
     def across(bundle, part):
         send(w_mine.at[bundle, cores[part], :], w_other.at[bundle, cores[part], :], c_sem.at[bundle, part], partner)
 
-    for part in range(2):
+    for part in range(4):
         onward(z, 1, 0, part)
         onward(z, 1, 1, part)
     for part in range(2):
         across(z, part)
 
-    for k in range(2):
-        is_remote = yl != 2 * c + k
-        rows = pl.ds(pl.multiple_of(RIM + 128 * k + 32 * x, 16), 32)
-        pl.when(is_remote)(lambda rows=rows, k=k: arrived(x_all.at[rows, :], a1_sem.at[k]))
-        for i in (1, 3, 2):
-            device = (ctx, 2 * lax.rem(x + i, 4) + c)
-            send(x_all.at[rows, :], x_all.at[rows, :], a2_sem.at[k, i - 1], device, is_remote)
-    for i in range(1, 8):
-        to = lax.rem(head + i, 8)
-        src = w_out.at[:, pl.ds(pl.multiple_of(256 * to, 256), 256)]
-        dst = wo_all.at[pl.ds(pl.multiple_of(256 * head, 256), 256), :]
-        send(src, dst, wo_sem.at[i - 1], (ctx, to))
+    tokens_out()
+    def tokens_on():
+        for k in range(2):
+            is_remote = yl != 2 * c + k
+            rows = pl.ds(pl.multiple_of(RIM + 128 * k + 32 * x, 16), 32)
+            pl.when(is_remote)(lambda rows=rows, k=k: arrived(x_all.at[rows, :], a1_sem.at[k]))
+            for i in (1, 3, 2):
+                device = (ctx, 2 * lax.rem(x + i, 4) + c)
+                send(x_all.at[rows, :], x_all.at[rows, :], a2_sem.at[k, i - 1], device, is_remote)
+        for i in range(1, 8):
+            to = lax.rem(head + i, 8)
+            src = w_out.at[:, pl.ds(pl.multiple_of(256 * to, 256), 256)]
+            dst = wo_all.at[pl.ds(pl.multiple_of(256 * head, 256), 256), :]
+            send(src, dst, wo_sem.at[i - 1], (ctx, to))
 
     def all_tokens():
         for k in range(2):
@@ -284,27 +323,34 @@
         for part in range(2):
             arrived(w_other.at[bundle, cores[part], :], c_sem.at[bundle, part])
         for which, weights in ((c, w_mine), (1 - c, w_other)):
-            product = dot(rows, weights[bundle, :256, :], precision=None)
+            product = dot(rows, weights[bundle, :256, :])
             acc[which] = product if first else acc[which] + product
-        small = dot(rows, w_mine[bundle, 256:272, :], ((1,), (1,)), precision=None)
+        small = dot(rows, w_mine[bundle, 256:272, :], ((1,), (1,)))
         logit[...] = small if first else logit[...] + small
 
     for step in range(1, 5):
         below, above = lax.rem(z + 8 - step, 8), lax.rem(z + step, 8)
-        for part in range(2):
+        for part in range(4):
             for way, bundle in ((0, below), (1, above)):
-                if step == 4 and part != way:
+                if step == 4 and part // 2 != way:
                     continue
                 arrived(w_mine.at[bundle, chunks[part], :], z_sem.at[way, step - 1, part])
-                if step < 3 or (step == 3 and part == way):
+                if step < 3 or (step == 3 and part // 2 == way):
                     onward(bundle, step + 1, way, part)
-                across(bundle, part)
+                if part % 2 == 1:
+                    across(bundle, part // 2)
         if step == 1:
+            tokens_on()
+        if step == 3:
             all_tokens()
             multiply(z, True)
-        multiply(below, False)
-        if step < 4:
-            multiply(above, False)
+            for near in range(1, 3):
+                multiply(lax.rem(z + 8 - near, 8), False)
+                multiply(lax.rem(z + near, 8), False)
+        if step >= 3:
+            multiply(below, False)
+            if step < 4:
+                multiply(above, False)
 
     arrived(p_other, par_sem)
     settings = jnp.where(hl // 2 == c, p_mine[...], p_other[...])
@@ -334,16 +380,14 @@
     softplus = jnp.maximum(shifted, 0.0) + jnp.log1p(jnp.exp(-jnp.abs(shifted)))
     decay = -pick(16, 18) * softplus
 
-    states, outputs = [], []
-    for b in range(2):
-        rows = slice(BLOCK * b, BLOCK * b + BLOCK)
-        state, solved, ratio, lead = block_state(
-            k_act[rows], v_act[rows], beta[rows], decay[rows], start[rows] - BLOCK * b
-        )
-        states.append(state)
-        outputs.append((solved, ratio, lead))
+    def blocks(array):
+        return [array[:BLOCK], array[BLOCK:]]
+
+    q_two, k_two, start_two = blocks(q_act), blocks(k_act), blocks(start)
+    states, solved, ratio, lead = block_states(
+        k_two, blocks(v_act), blocks(beta), blocks(decay), [start_two[0], start_two[1] - BLOCK]
+    )
     z_unit[...] = compose(states[0], states[1])
-    z_copy = len(pending)
     send(z_unit, z_first, zf_sem, partner, c == 0)
 
     targets = [(place(group + d, hl), head) for d in range(1, 5)]
@@ -356,27 +400,28 @@
 
     for d in range(4):
         part = pl.ds(0, size[d])
-        send(z_send.at[part, :], z_in.at[d, part, :], zi_sem.at[d], targets[d], c == 1)
-
-    leads, rests = [], []
-    for b in range(2):
-        rows = slice(BLOCK * b, BLOCK * b + BLOCK)
-        lead_part, rest = block_output(q_act[rows], k_act[rows], *outputs[b])
-        if b == 1:
-            through = dot(lead_part, states[0], ((1,), (1,)))
-            lead_part, rest = through[:, HD:], rest + through[:, :HD]
-        leads.append(lead_part)
-        rests.append(rest)
+        send(z_send.at[:, part], z_in.at[d, :, part], zi_sem.at[d], targets[d], c == 1)
+
+    scores = each(lambda q, k, ratio: dot3(q, k.T) * ratio, q_two, k_two, ratio)
+    mixed = each(dot3, scores, solved)
+    leads = each(lambda q, lead, mixed: lead * q - mixed[:, HD:], q_two, lead, mixed)
+    rests = each(lambda mixed: mixed[:, :HD], mixed)
+    through = dot3(leads[1], states[0])
+    leads[1], rests[1] = through[:, HD:], rests[1] + through[:, :HD]
+    lead_all, rest_all = jnp.concatenate(leads, axis=0), jnp.concatenate(rests, axis=0)
     gate = acc[1, RIM:, HD:]
     gate = gate * sigmoid(gate) * gain[...]
+    done = len(pending) - 5
+    for copy, cond in pending[:done]:
+        sent(copy, cond)
 
     @pl.when(c == 1)
     def _():
         for d in range(4):
-            arrived(z_in.at[d, pl.ds(0, size[d]), :], zi_sem.at[d])
-        state = z_in[3, :HD].astype(F32)
+            arrived(z_in.at[d, :, pl.ds(0, size[d])], zi_sem.at[d])
+        state = z_in[3, :, :HD].astype(F32)
         for d in (2, 1, 0):
-            state = dot(state, z_in[d, HD:].astype(F32)) + z_in[d, :HD].astype(F32)
+            state = dot2(z_in[d, :, HD:], state) + z_in[d, :, :HD].astype(F32)
         s_in[0] = state
 
     send(s_in.at[0], s_in.at[1], si_sem, partner, c == 1)
@@ -384,10 +429,10 @@
 
     @pl.when(c == 1)
     def _():
-        s_in[1] = dot(s_in[0], z_first[HD:, :]) + z_first[:HD, :]
+        s_in[1] = dot3(z_first[:, HD:], s_in[0]) + z_first[:, :HD]
 
     before = s_in[1]
-    result = dot(jnp.concatenate(leads, axis=0), before, ((1,), (1,))) + jnp.concatenate(rests, axis=0)
+    result = dot3(lead_all, before) + rest_all
     scale = lax.rsqrt(jnp.mean(result * result, axis=1, keepdims=True) + EPSILON)
     n_stage[...] = (result * scale * gate).astype(BF16)
 
@@ -422,14 +467,11 @@
     total = jnp.zeros((128, 256), F32)
     for i in range(8):
         rows = jnp.concatenate([n_all[2 * i], n_all[2 * i + 1]], axis=1)
-        total = total + dot(rows, wo_all[256 * i : 256 * i + 256, :], precision=None)
+        total = total + dot(rows, wo_all[256 * i : 256 * i + 256, :])
     out[...] = total.astype(BF16)
 
-    for copy, cond in pending:
-        if cond is None:
-            copy.wait_send()
-        else:
-            pl.when(cond)(copy.wait_send)
+    for copy, cond in pending[done:]:
+        sent(copy, cond)
 
 
 def local(
@@ -462,20 +504,20 @@
             pltpu.VMEM((24, HD), F32),
             pltpu.VMEM((2, RIM + 256, 256), F32),
             pltpu.VMEM((RIM + 256, 16), F32),
-            pltpu.VMEM((2 * HD, HD), F32),
-            pltpu.VMEM((2 * HD, HD), F32),
-            pltpu.VMEM((2 * HD, HD), BF16),
-            pltpu.VMEM((4, 2 * HD, HD), BF16),
+            pltpu.VMEM((HD, 2 * HD), F32),
+            pltpu.VMEM((HD, 2 * HD), F32),
+            pltpu.VMEM((HD, 2 * HD), BF16),
+            pltpu.VMEM((4, HD, 2 * HD), BF16),
             pltpu.VMEM((2, HD, HD), F32),
             pltpu.VMEM((256, HD), BF16),
             pltpu.VMEM((16, 128, HD), BF16),
-            dma((110,)),
+            dma((128,)),
             dma((2,)),
             dma((2, 3)),
             dma,
             dma((8,)),
             dma((8,)),
-            dma((2, 4, 2)),
+            dma((2, 4, 4)),
             dma((8, 2)),
             dma((7,)),
             dma,

time: 80.9 us -> 73.9 us (0.913)
  Pallas kernels: 79.2 us -> 72.2 us
    pallas_call x1, Pallas kernels: 79.2 us -> 72.2 us  [local(): pl.pallas_call(kernel, out_shape=jax.ShapeDtypeStruct((128, 256), BF16),...]
where the time goes in v3:
time: 73.9 us; the launch traced here: 73.7 us
  Pallas kernels  72.2 us (98%)
  local copies, waits for them, and re-layouts  1.47 us (2%)
    pallas_call x1, Pallas kernels, local(): pl.pallas_call(kernel, out_shape=jax.ShapeDtypeStruct((128, 256), BF16),...  72.2 us

profile of v3, /device:TPU:1, one launch (start us, length us, event | category | flops | bytes accessed | tf_op | source)
XLA Modules:
  0.0 73.7 jit_solution(8213070992292671857)
XLA Ops:
  0.0 72.2 %shard_map.136 = bf16[128,256]{1,0:T(8,128)(2,1)} custom-call(bf16[128,2048]{1,0:T(8,128)(2,1)} %tokens.1, bf16[32,128]{1,0:T(8,128)(2,1)} %w_query.1, bf16[32,128]{1,0:T(8,128)(2,1)} %w_key.1, bf16[32,256]{1,0:T(8,128)(2,1)} %w_value.1, bf16[32,256]{1,0:T(8,128)(2,1)} %w_gate.1, bf16[2,32]{1,0:T(2,128)(2,1)} %bitcast.3, bf16[2,32]{1,0:T(2,128)(2,1)} %bitcast.4, ...), custom_call_target="tpu_custom_call" | custom-call | tf_op jit(solution)/shard_map/pallas_call | solution.py:483
  72.2 1.5 %copy.16 = bf16[128,256]{1,0:T(8,128)(2,1)} copy(bf16[128,256]{1,0:T(8,128)(2,1)} %shard_map.136) | data formatting | bytes 131072

commit v4 on v3

--- a/solution.py
+++ b/solution.py
@@ -143,28 +143,6 @@
     def arrived(dst, sem):
         pltpu.make_async_copy(dst, dst, sem).wait()
 
-    barrier = pltpu.get_barrier_semaphore()
-
-    def greet(device):
-        pl.semaphore_signal(barrier, inc=1, device_id=device, device_id_type=MESH)
-
-    for i in range(1, 8):
-        other = 8 * z + lax.rem(y + i, 8)
-        greet((other, 2 * x))
-        greet((other, 2 * x + 1))
-    for i in range(1, 8):
-        greet((ctx, lax.rem(head + i, 8)))
-    greet((lax.rem(ctx + 8, 64), head))
-    greet((lax.rem(ctx + 56, 64), head))
-    pl.when((c == 0) & (yh == 0))(lambda: greet((lax.rem(4 * group + 63, 64), 2 * x + 1)))
-
-    @pl.when(c == 1)
-    def _():
-        for d in range(1, 5):
-            greet((place(group - d, hl), head))
-
-    rim_across = (c == 1) & (y == 7)
-
     inputs = [
         pltpu.make_async_copy(src, dst, in_sem.at[i])
         for i, (src, dst) in enumerate(
@@ -186,19 +164,36 @@
             ]
         )
     ]
-    for copy in inputs:
+    for copy in inputs[:8]:
         copy.start()
 
-    for copy in inputs:
+    barrier = pltpu.get_barrier_semaphore()
+
+    def greet(device):
+        pl.semaphore_signal(barrier, inc=1, device_id=device, device_id_type=MESH)
+
+    for i in range(1, 8):
+        other = 8 * z + lax.rem(y + i, 8)
+        greet((other, 2 * x))
+        greet((other, 2 * x + 1))
+    for i in range(1, 8):
+        greet((ctx, lax.rem(head + i, 8)))
+    greet((lax.rem(ctx + 8, 64), head))
+    greet((lax.rem(ctx + 56, 64), head))
+    pl.when((c == 0) & (yh == 0))(lambda: greet((lax.rem(4 * group + 63, 64), 2 * x + 1)))
+
+    @pl.when(c == 1)
+    def _():
+        for d in range(1, 5):
+            greet((place(group - d, hl), head))
+
+    rim_across = (c == 1) & (y == 7)
+
+    for copy in inputs[8:]:
+        copy.start()
+
+    for copy in inputs[:8]:
         copy.wait()
-    for s in range(4):
-        for i in range(2):
-            p_mine[2 * s + i : 2 * s + i + 1, :] = conv_qk[s, i : i + 1, :]
-        for i in range(2):
-            p_mine[8 + 4 * i + s : 9 + 4 * i + s, :] = conv_value[s : s + 1, HD * i : HD * i + HD]
-    for i in range(2):
-        p_mine[16 + 2 * i : 17 + 2 * i, :] = jnp.full((1, HD), rate[i], F32)
-        p_mine[17 + 2 * i : 18 + 2 * i, :] = jnp.full((1, HD), bias[i], F32)
     piece[...] = jnp.zeros((16, HD), BF16)
     for q in range(4):
 
@@ -209,7 +204,7 @@
 
     pl.semaphore_wait(barrier, 23 + 4 * c + 4 * rim_across.astype(jnp.int32))
 
-    mine_rows = pl.ds(pl.multiple_of(32 * y, 32), 32)
+    mine_rows = pl.ds(pl.multiple_of(80 * (y // 2) + 32 * (y % 2), 16), 32)
     selfs = []
     for sub in range(2):
         local = 2 * c + sub
@@ -231,20 +226,36 @@
             pltpu.make_async_copy(src, dst, y_sem.at[y]).start()
             pltpu.make_async_copy(piece, pieces.at[y], p_sem.at[y]).start()
 
+    quarter = pl.ds(pl.multiple_of(32 * x, 32), 32)
+    lanes = [pl.ds(1024 * i, 1024) for i in range(2)]
+    rim_lanes = pl.ds(pl.multiple_of(512 * x, 512), 512)
+
     def tokens_out():
-        quarter = pl.ds(pl.multiple_of(32 * x, 32), 32)
         owner = yl // 2 == c
-        for i in range(1, 4):
-            to = 4 * group + lax.rem(yl + i, 4)
-            rows = pl.ds(pl.multiple_of(RIM + 128 * (yl % 2) + 32 * x, 16), 32)
-            send(tokens.at[quarter, :], x_all.at[rows, :], a1_sem.at[yl % 2], (to, head), owner)
+        rows = pl.ds(pl.multiple_of(RIM + 128 * (yl % 2) + 32 * x, 16), 32)
+        for i in range(2):
+            for j in range(1, 4):
+                to = 4 * group + lax.rem(yl + j, 4)
+                dst = x_all.at[rows, lanes[i]]
+                send(tokens.at[quarter, lanes[i]], dst, a1_sem.at[yl % 2, i], (to, head), owner)
         after_two = (c == 0) & (yl == 1)
         after_four = (c == 1) & (yl == 3)
-        for i in range(4):
-            last = tokens.at[pl.ds(128 - RIM, RIM), :]
-            to = jnp.where(after_two, 4 * group + i, lax.rem(4 * group + 4 + i, 64))
-            send(last, x_all.at[pl.ds(0, RIM), :], rim_sem, (to, 2 * x + 1 - c), after_two | after_four)
-
+        for j in range(4):
+            last = tokens.at[pl.ds(128 - RIM, RIM), rim_lanes]
+            to = jnp.where(after_two, 4 * group + j, lax.rem(4 * group + 4 + j, 64))
+            dst = x_all.at[pl.ds(0, RIM), rim_lanes]
+            send(last, dst, rim_sem.at[0], (to, 2 * x + 1 - c), after_two | after_four)
+
+    for copy in inputs[8:]:
+        copy.wait()
+    for s in range(4):
+        for i in range(2):
+            p_mine[2 * s + i : 2 * s + i + 1, :] = conv_qk[s, i : i + 1, :]
+        for i in range(2):
+            p_mine[8 + 4 * i + s : 9 + 4 * i + s, :] = conv_value[s : s + 1, HD * i : HD * i + HD]
+    for i in range(2):
+        p_mine[16 + 2 * i : 17 + 2 * i, :] = jnp.full((1, HD), rate[i], F32)
+        p_mine[17 + 2 * i : 18 + 2 * i, :] = jnp.full((1, HD), bias[i], F32)
     send(p_mine, p_other, par_sem, partner)
     own_block = []
     for k in range(2):
@@ -267,67 +278,80 @@
         start = jnp.maximum(start, jnp.where(place_of >= offset, offset, -FAR))
         offset = offset + docs[i]
 
-    for i in range(8):
-        arrived(w_mine.at[z, pl.ds(32 * i, 32), :], y_sem.at[i])
-        arrived(pieces.at[i], p_sem.at[i])
-    for i in range(2):
-        joined = sum(pieces[4 * i + j].astype(F32) for j in range(4))
-        w_mine[z, 256:272, HD * i : HD * i + HD] = joined.astype(BF16)
-
     ups, downs = lax.rem(ctx + 8, 64), lax.rem(ctx + 56, 64)
-    chunks = [pl.ds(at, size) for at, size in ((0, 80), (80, 64), (144, 64), (208, 64))]
-    cores = (pl.ds(0, 144), pl.ds(144, 112))
+    parts = [lax.rem(y // 2 + i, 4) for i in (0, 1, 3, 2)]
+    chunks = [pl.ds(pl.multiple_of(80 * part, 16), 64 if i < 3 else 80) for i, part in enumerate(parts)]
+    narrow = [pl.ds(pl.multiple_of(80 * part, 16), 64) for part in parts]
+    extra = pl.ds(pl.multiple_of(80 * parts[3] + 64, 16), 16)
 
     def onward(bundle, step, way, part):
         ref = w_mine.at[bundle, chunks[part], :]
         send(ref, ref, z_sem.at[way, step - 1, part], (ups if way == 0 else downs, head))
 
     def across(bundle, part):
-        send(w_mine.at[bundle, cores[part], :], w_other.at[bundle, cores[part], :], c_sem.at[bundle, part], partner)
+        ref = narrow[part]
+        send(w_mine.at[bundle, ref, :], w_other.at[bundle, ref, :], c_sem.at[bundle, part], partner)
 
     for part in range(4):
+        for i in range(2):
+            chip = 2 * parts[part] + i
+            arrived(w_mine.at[z, pl.ds(pl.multiple_of(80 * parts[part] + 32 * i, 16), 32), :], y_sem.at[chip])
+            arrived(pieces.at[chip], p_sem.at[chip])
+        if part == 3:
+            for i in range(2):
+                joined = sum(pieces[4 * i + j].astype(F32) for j in range(4))
+                w_mine[z, extra, HD * i : HD * i + HD] = joined.astype(BF16)
         onward(z, 1, 0, part)
         onward(z, 1, 1, part)
-    for part in range(2):
+        if part == 0:
+            tokens_out()
         across(z, part)
 
-    tokens_out()
-    def tokens_on():
+    def tokens_on(i):
         for k in range(2):
             is_remote = yl != 2 * c + k
             rows = pl.ds(pl.multiple_of(RIM + 128 * k + 32 * x, 16), 32)
-            pl.when(is_remote)(lambda rows=rows, k=k: arrived(x_all.at[rows, :], a1_sem.at[k]))
-            for i in (1, 3, 2):
-                device = (ctx, 2 * lax.rem(x + i, 4) + c)
-                send(x_all.at[rows, :], x_all.at[rows, :], a2_sem.at[k, i - 1], device, is_remote)
-        for i in range(1, 8):
-            to = lax.rem(head + i, 8)
-            src = w_out.at[:, pl.ds(pl.multiple_of(256 * to, 256), 256)]
-            dst = wo_all.at[pl.ds(pl.multiple_of(256 * head, 256), 256), :]
-            send(src, dst, wo_sem.at[i - 1], (ctx, to))
+            ref = x_all.at[rows, lanes[i]]
+            pl.when(is_remote)(lambda ref=ref, k=k: arrived(ref, a1_sem.at[k, i]))
+            for j in (1, 3, 2):
+                send(ref, ref, a2_sem.at[k, j - 1, i], (ctx, 2 * lax.rem(x + j, 4) + c), is_remote)
+
+    def rim_on():
+        ref = x_all.at[pl.ds(0, RIM), rim_lanes]
+        arrived(ref, rim_sem.at[0])
+        for j in (1, 3, 2):
+            send(ref, ref, rim_sem.at[j], (ctx, 2 * lax.rem(x + j, 4) + c))
 
     def all_tokens():
         for k in range(2):
 
             @pl.when(yl != 2 * c + k)
             def _(k=k):
-                for i in range(1, 4):
-                    rows = pl.ds(pl.multiple_of(RIM + 128 * k + 32 * lax.rem(x + 4 - i, 4), 16), 32)
-                    arrived(x_all.at[rows, :], a2_sem.at[k, i - 1])
+                for i in range(2):
+                    for j in range(1, 4):
+                        rows = pl.ds(pl.multiple_of(RIM + 128 * k + 32 * lax.rem(x + 4 - j, 4), 16), 32)
+                        arrived(x_all.at[rows, lanes[i]], a2_sem.at[k, j - 1, i])
 
             pl.when(own_block[k][0])(own_block[k][1].wait)
-        arrived(x_all.at[pl.ds(0, RIM), :], rim_sem)
+        for j in range(1, 4):
+            there = pl.ds(pl.multiple_of(512 * lax.rem(x + 4 - j, 4), 512), 512)
+            arrived(x_all.at[pl.ds(0, RIM), there], rim_sem.at[j])
 
     def multiply(bundle, first):
         rows = x_all[:, pl.ds(pl.multiple_of(256 * bundle, 256), 256)]
-        for part in range(2):
-            arrived(w_other.at[bundle, cores[part], :], c_sem.at[bundle, part])
-        for which, weights in ((c, w_mine), (1 - c, w_other)):
-            product = dot(rows, weights[bundle, :256, :])
+
+        def add(which, weights):
+            product = dot(rows, jnp.concatenate([weights[bundle, 80 * i : 80 * i + 64, :] for i in range(4)], axis=0))
             acc[which] = product if first else acc[which] + product
-        small = dot(rows, w_mine[bundle, 256:272, :], ((1,), (1,)))
+
+        add(c, w_mine)
+        small = dot(rows, w_mine[bundle, extra, :], ((1,), (1,)))
         logit[...] = small if first else logit[...] + small
-
+        for part in range(4):
+            arrived(w_other.at[bundle, narrow[part], :], c_sem.at[bundle, part])
+        add(1 - c, w_other)
+
+    tokens_on(0)
     for step in range(1, 5):
         below, above = lax.rem(z + 8 - step, 8), lax.rem(z + step, 8)
         for part in range(4):
@@ -337,10 +361,11 @@
                 arrived(w_mine.at[bundle, chunks[part], :], z_sem.at[way, step - 1, part])
                 if step < 3 or (step == 3 and part // 2 == way):
                     onward(bundle, step + 1, way, part)
-                if part % 2 == 1:
-                    across(bundle, part // 2)
+                across(bundle, part)
         if step == 1:
-            tokens_on()
+            tokens_on(1)
+        if step == 1:
+            rim_on()
         if step == 3:
             all_tokens()
             multiply(z, True)
@@ -351,6 +376,12 @@
             multiply(below, False)
             if step < 4:
                 multiply(above, False)
+
+    for i in range(1, 8):
+        to = lax.rem(head + i, 8)
+        src = w_out.at[:, pl.ds(pl.multiple_of(256 * to, 256), 256)]
+        dst = wo_all.at[pl.ds(pl.multiple_of(256 * head, 256), 256), :]
+        send(src, dst, wo_sem.at[i - 1], (ctx, to))
 
     arrived(p_other, par_sem)
     settings = jnp.where(hl // 2 == c, p_mine[...], p_other[...])
@@ -398,7 +429,7 @@
         arrived(z_first, zf_sem)
         z_send[...] = compose(z_first[...], z_unit[...]).astype(BF16)
 
-    for d in range(4):
+    for d in (2, 3, 0, 1):
         part = pl.ds(0, size[d])
         send(z_send.at[:, part], z_in.at[d, :, part], zi_sem.at[d], targets[d], c == 1)
 
@@ -494,8 +525,8 @@
             pltpu.VMEM((1, HD), F32),
             pltpu.SMEM((32,), jnp.int32),
             pltpu.VMEM((RIM + 256, 2048), BF16),
-            pltpu.VMEM((8, 272, 256), BF16),
-            pltpu.VMEM((8, 256, 256), BF16),
+            pltpu.VMEM((8, 320, 256), BF16),
+            pltpu.VMEM((8, 320, 256), BF16),
             pltpu.VMEM((2048, 256), BF16),
             pltpu.VMEM((3, 32, 256), BF16),
             pltpu.VMEM((16, HD), BF16),
@@ -511,14 +542,14 @@
             pltpu.VMEM((2, HD, HD), F32),
             pltpu.VMEM((256, HD), BF16),
             pltpu.VMEM((16, 128, HD), BF16),
-            dma((128,)),
-            dma((2,)),
-            dma((2, 3)),
-            dma,
+            dma((144,)),
+            dma((2, 2)),
+            dma((2, 3, 2)),
+            dma((4,)),
             dma((8,)),
             dma((8,)),
             dma((2, 4, 4)),
-            dma((8, 2)),
+            dma((8, 4)),
             dma((7,)),
             dma,
             dma,

time: 73.9 us -> 65.3 us (0.88)
  Pallas kernels: 72.2 us -> 63.6 us
    pallas_call x1, Pallas kernels: 72.2 us -> 63.6 us  [local(): pl.pallas_call(kernel, out_shape=jax.ShapeDtypeStruct((128, 256), BF16),...]
where the time goes in v4:
time: 65.3 us; the launch traced here: 65.1 us
  Pallas kernels  63.6 us (97%)
  local copies, waits for them, and re-layouts  1.47 us (2%)
    pallas_call x1, Pallas kernels, local(): pl.pallas_call(kernel, out_shape=jax.ShapeDtypeStruct((128, 256), BF16),...  63.6 us
    unnamed x1, local copies, waits for them, and re-layouts  1.47 us

profile of v4, /device:TPU:1, one launch (start us, length us, event | category | flops | bytes accessed | tf_op | source)
XLA Modules:
  0.0 65.1 jit_solution(17736296458510668818)
XLA Ops:
  0.0 63.6 %shard_map.136 = bf16[128,256]{1,0:T(8,128)(2,1)} custom-call(bf16[128,2048]{1,0:T(8,128)(2,1)} %tokens.1, bf16[32,128]{1,0:T(8,128)(2,1)} %w_query.1, bf16[32,128]{1,0:T(8,128)(2,1)} %w_key.1, bf16[32,256]{1,0:T(8,128)(2,1)} %w_value.1, bf16[32,256]{1,0:T(8,128)(2,1)} %w_gate.1, bf16[2,32]{1,0:T(2,128)(2,1)} %bitcast.3, bf16[2,32]{1,0:T(2,128)(2,1)} %bitcast.4, ...), custom_call_target="tpu_custom_call" | custom-call | tf_op jit(solution)/shard_map/pallas_call | solution.py:514
  63.6 1.5 %copy.16 = bf16[128,256]{1,0:T(8,128)(2,1)} copy(bf16[128,256]{1,0:T(8,128)(2,1)} %shard_map.136) | data formatting | bytes 131072

commit v5 on v4

--- a/solution.py
+++ b/solution.py
@@ -296,8 +296,9 @@
         for i in range(2):
             chip = 2 * parts[part] + i
             arrived(w_mine.at[z, pl.ds(pl.multiple_of(80 * parts[part] + 32 * i, 16), 32), :], y_sem.at[chip])
-            arrived(pieces.at[chip], p_sem.at[chip])
         if part == 3:
+            for i in range(8):
+                arrived(pieces.at[i], p_sem.at[i])
             for i in range(2):
                 joined = sum(pieces[4 * i + j].astype(F32) for j in range(4))
                 w_mine[z, extra, HD * i : HD * i + HD] = joined.astype(BF16)
@@ -372,16 +373,16 @@
             for near in range(1, 3):
                 multiply(lax.rem(z + 8 - near, 8), False)
                 multiply(lax.rem(z + near, 8), False)
-        if step >= 3:
-            multiply(below, False)
-            if step < 4:
-                multiply(above, False)
-
     for i in range(1, 8):
         to = lax.rem(head + i, 8)
         src = w_out.at[:, pl.ds(pl.multiple_of(256 * to, 256), 256)]
         dst = wo_all.at[pl.ds(pl.multiple_of(256 * head, 256), 256), :]
         send(src, dst, wo_sem.at[i - 1], (ctx, to))
+
+    for near in range(3, 5):
+        multiply(lax.rem(z + 8 - near, 8), False)
+        if near < 4:
+            multiply(lax.rem(z + near, 8), False)
 
     arrived(p_other, par_sem)
     settings = jnp.where(hl // 2 == c, p_mine[...], p_other[...])
@@ -439,7 +440,6 @@
     rests = each(lambda mixed: mixed[:, :HD], mixed)
     through = dot3(leads[1], states[0])
     leads[1], rests[1] = through[:, HD:], rests[1] + through[:, :HD]
-    lead_all, rest_all = jnp.concatenate(leads, axis=0), jnp.concatenate(rests, axis=0)
     gate = acc[1, RIM:, HD:]
     gate = gate * sigmoid(gate) * gain[...]
     done = len(pending) - 5
@@ -463,12 +463,12 @@
         s_in[1] = dot3(z_first[:, HD:], s_in[0]) + z_first[:, :HD]
 
     before = s_in[1]
-    result = dot3(lead_all, before) + rest_all
-    scale = lax.rsqrt(jnp.mean(result * result, axis=1, keepdims=True) + EPSILON)
-    n_stage[...] = (result * scale * gate).astype(BF16)
-
     my_head = 4 * x + hl
     for b in range(2):
+        rows = slice(BLOCK * b, BLOCK * b + BLOCK)
+        result = dot3(leads[b], before) + rests[b]
+        scale = lax.rsqrt(jnp.mean(result * result, axis=1, keepdims=True) + EPSILON)
+        n_stage[rows, :] = (result * scale * gate[rows]).astype(BF16)
         src = n_stage.at[pl.ds(BLOCK * b, BLOCK), :]
         dst = n_all.at[my_head]
         is_self = (yl == 2 * c + b) & (hl % 2 == c)
@@ -513,7 +513,7 @@
     dma = pltpu.SemaphoreType.DMA
     return pl.pallas_call(
         kernel,
-        out_shape=jax.ShapeDtypeStruct((128, 256), BF16),
+        out_shape=pltpu.VMEM((128, 256), BF16),
         in_specs=[pl.BlockSpec(memory_space=pltpu.HBM)] * 14,
         out_specs=vmem,
         scratch_shapes=[

time: 65.3 us -> 63 us (0.965)
  Pallas kernels: 63.6 us -> 62.2 us
  local copies, waits for them, and re-layouts: 1.47 us -> 0.63 us
    pallas_call x1, Pallas kernels: 63.6 us -> 62.2 us  [local(): pl.pallas_call(kernel, out_shape=pltpu.VMEM((128, 256), BF16), in_specs=[...]
    unnamed x1, local copies, waits for them, and re-layouts: 1.47 us -> 0.63 us
where the time goes in v5:
time: 63 us; the launch traced here: 62.9 us
  Pallas kernels  62.2 us (99%)
  local copies, waits for them, and re-layouts  0.63 us (1%)
    pallas_call x1, Pallas kernels, local(): pl.pallas_call(kernel, out_shape=pltpu.VMEM((128, 256), BF16), in_specs=[...  62.2 us

profile of v5, /device:TPU:1, one launch (start us, length us, event | category | flops | bytes accessed | tf_op | source)
XLA Modules:
  0.0 62.9 jit_solution(11895472667426853860)
XLA Ops:
  0.0 62.2 %shard_map.136 = bf16[128,256]{1,0:T(8,128)(2,1)S(1)} custom-call(bf16[128,2048]{1,0:T(8,128)(2,1)} %tokens.1, bf16[32,128]{1,0:T(8,128)(2,1)} %w_query.1, bf16[32,128]{1,0:T(8,128)(2,1)} %w_key.1, bf16[32,256]{1,0:T(8,128)(2,1)} %w_value.1, bf16[32,256]{1,0:T(8,128)(2,1)} %w_gate.1, bf16[2,32]{1,0:T(2,128)(2,1)} %bitcast.3, bf16[2,32]{1,0:T(2,128)(2,1)} %bitcast.4, ...), custom_call_target="tpu_custom_call" | custom-call | tf_op jit(solution)/shard_map/pallas_call | solution.py:514
  62.2 0.6 %copy.16 = bf16[128,256]{1,0:T(8,128)(2,1)} copy(bf16[128,256]{1,0:T(8,128)(2,1)S(1)} %shard_map.136) | data formatting | bytes 131072

commit v6 on v5

--- a/solution.py
+++ b/solution.py
@@ -101,10 +101,10 @@
 
 
 def kernel(
-    tokens, w_query, w_key, w_value, w_gate, w_beta, w_decay, rate_in, bias_in, conv_qk_in, conv_value_in, gain_in, w_out,
+    tokens, w_query, w_key, w_value, w_gate, w_small, rate_in, bias_in, conv_qk_in, conv_value_in, gain_in, w_out,
     docs_in,
     out,
-    beta_w, rate, bias, conv_qk, conv_value, gain, docs,
+    small_w, rate, bias, conv_qk, conv_value, gain, docs,
     x_all, w_mine, w_other, wo_all, w_stage, piece, pieces, p_mine, p_other, acc, logit,
     z_unit, z_first, z_send, z_in, s_in, n_stage, n_all,
     send_sem, a1_sem, a2_sem, rim_sem, y_sem, p_sem, z_sem, c_sem, wo_sem, par_sem, zf_sem, zi_sem, si_sem, n_sem, own_sem,
@@ -153,8 +153,7 @@
                 (w_value.at[:, HD:], w_stage.at[2, :, :HD]),
                 (w_gate.at[:, :HD], w_stage.at[1, :, HD:]),
                 (w_gate.at[:, HD:], w_stage.at[2, :, HD:]),
-                (w_beta, beta_w.at[0]),
-                (w_decay, beta_w.at[1]),
+                (w_small, small_w),
                 (rate_in, rate),
                 (bias_in, bias),
                 (conv_qk_in, conv_qk),
@@ -164,7 +163,7 @@
             ]
         )
     ]
-    for copy in inputs[:8]:
+    for copy in inputs[:7]:
         copy.start()
 
     barrier = pltpu.get_barrier_semaphore()
@@ -189,18 +188,17 @@
 
     rim_across = (c == 1) & (y == 7)
 
-    for copy in inputs[8:]:
+    for copy in inputs[7:]:
         copy.start()
 
-    for copy in inputs[:8]:
+    for copy in inputs[:7]:
         copy.wait()
     piece[...] = jnp.zeros((16, HD), BF16)
     for q in range(4):
 
         @pl.when(y % 4 == q)
         def _(q=q):
-            piece[0:2, 32 * q : 32 * q + 32] = beta_w[0]
-            piece[2:4, 32 * q : 32 * q + 32] = beta_w[1]
+            piece[0:4, 32 * q : 32 * q + 32] = small_w[...].astype(BF16)
 
     pl.semaphore_wait(barrier, 23 + 4 * c + 4 * rim_across.astype(jnp.int32))
 
@@ -246,7 +244,7 @@
             dst = x_all.at[pl.ds(0, RIM), rim_lanes]
             send(last, dst, rim_sem.at[0], (to, 2 * x + 1 - c), after_two | after_four)
 
-    for copy in inputs[8:]:
+    for copy in inputs[7:]:
         copy.wait()
     for s in range(4):
         for i in range(2):
@@ -510,14 +508,15 @@
     w_out, doc_lengths,
 ):
     vmem = pl.BlockSpec(memory_space=pltpu.VMEM)
+    small = jnp.concatenate([w_beta.T, w_decay.T], axis=0).astype(F32)
     dma = pltpu.SemaphoreType.DMA
     return pl.pallas_call(
         kernel,
         out_shape=pltpu.VMEM((128, 256), BF16),
-        in_specs=[pl.BlockSpec(memory_space=pltpu.HBM)] * 14,
+        in_specs=[pl.BlockSpec(memory_space=pltpu.HBM)] * 13,
         out_specs=vmem,
         scratch_shapes=[
-            pltpu.VMEM((2, 2, 32), BF16),
+            pltpu.VMEM((4, 32), F32),
             pltpu.SMEM((2,), F32),
             pltpu.SMEM((2,), F32),
             pltpu.VMEM((4, 2, HD), F32),
@@ -557,13 +556,13 @@
             dma,
             dma((16,)),
             dma((2,)),
-            dma((14,)),
+            dma((13,)),
         ],
         compiler_params=pltpu.CompilerParams(
             collective_id=0, has_side_effects=True, vmem_limit_bytes=60 * 2**20
         ),
     )(
-        tokens, w_query, w_key, w_value, w_output_gate, w_beta.T, w_decay.T, decay_rate, dt_bias, conv_qk, conv_value,
+        tokens, w_query, w_key, w_value, w_output_gate, small, decay_rate, dt_bias, conv_qk, conv_value,
         norm_gain.reshape(1, HD), w_out, doc_lengths,
     )
 

time: 63 us -> 64.3 us (1.021)
  local copies, waits for them, and re-layouts: 0.63 us -> 1.3 us
    unnamed x1 -> x5, local copies, waits for them, and re-layouts: 0.63 us -> 1.3 us
where the time goes in v6:
time: 64.3 us; the launch traced here: 64.1 us
  Pallas kernels  62.2 us (97%)
  local copies, waits for them, and re-layouts  1.3 us (2%)
    pallas_call x1, Pallas kernels, local(): pl.pallas_call(kernel, out_shape=pltpu.VMEM((128, 256), BF16), in_specs=[...  62.2 us
    unnamed x5, local copies, waits for them, and re-layouts  1.3 us

profile of v6, /device:TPU:1, one launch (start us, length us, event | category | flops | bytes accessed | tf_op | source)
XLA Modules:
  0.0 64.1 jit_solution(15966375000975243744)
XLA Ops:
  0.0 0.0 copy-start
  0.0 0.0 copy-start.1
  0.0 0.7 %copy-done = bf16[32,2]{0,1:T(2,128)(2,1)S(1)} copy-done((bf16[32,2]{0,1:T(2,128)(2,1)S(1)}, bf16[32,2]{0,1:T(2,128)(2,1)}, u32[]{:S(2)}) %copy-start) | copy-done | bytes 152
  0.7 0.0 copy-done.1
  0.7 0.6 maximum_convert_fusion.w_small
  1.3 62.2 %shard_map.136 = bf16[128,256]{1,0:T(8,128)(2,1)S(1)} custom-call(bf16[128,2048]{1,0:T(8,128)(2,1)} %tokens.1, bf16[32,128]{1,0:T(8,128)(2,1)} %w_query.1, bf16[32,128]{1,0:T(8,128)(2,1)} %w_key.1, bf16[32,256]{1,0:T(8,128)(2,1)} %w_value.1, bf16[32,256]{1,0:T(8,128)(2,1)} %w_gate.1, f32[4,32]{1,0:T(4,128)} %maximum_convert_fusion.w_small, f32[2]{0:T(128)} %rate_in.1, ...), custom_call_target="tpu_custom_call" | custom-call | tf_op jit(solution)/shard_map/pallas_call | solution.py:513
  63.5 0.6 copy.16
Async XLA Ops:
  0.0 0.7 %copy-start = (bf16[32,2]{0,1:T(2,128)(2,1)S(1)}, bf16[32,2]{0,1:T(2,128)(2,1)}, u32[]{:S(2)}) copy-start(bf16[32,2]{0,1:T(2,128)(2,1)} %param.20) | copy-start | bytes 388
  0.0 0.7 %copy-start.1 = (bf16[32,2]{0,1:T(2,128)(2,1)S(1)}, bf16[32,2]{0,1:T(2,128)(2,1)}, u32[]{:S(2)}) copy-start(bf16[32,2]{0,1:T(2,128)(2,1)} %param.19) | copy-start | bytes 388

commit v7 on v5

--- a/solution.py
+++ b/solution.py
@@ -104,7 +104,7 @@
     tokens, w_query, w_key, w_value, w_gate, w_beta, w_decay, rate_in, bias_in, conv_qk_in, conv_value_in, gain_in, w_out,
     docs_in,
     out,
-    beta_w, rate, bias, conv_qk, conv_value, gain, docs,
+    quarter_stage, rim_stage, beta_w, rate, bias, conv_qk, conv_value, gain, docs,
     x_all, w_mine, w_other, wo_all, w_stage, piece, pieces, p_mine, p_other, acc, logit,
     z_unit, z_first, z_send, z_in, s_in, n_stage, n_all,
     send_sem, a1_sem, a2_sem, rim_sem, y_sem, p_sem, z_sem, c_sem, wo_sem, par_sem, zf_sem, zi_sem, si_sem, n_sem, own_sem,
@@ -142,6 +142,9 @@
 
     def arrived(dst, sem):
         pltpu.make_async_copy(dst, dst, sem).wait()
+
+    quarter = pl.ds(pl.multiple_of(32 * x, 32), 32)
+    rim_lanes = pl.ds(pl.multiple_of(512 * x, 512), 512)
 
     inputs = [
         pltpu.make_async_copy(src, dst, in_sem.at[i])
@@ -161,6 +164,8 @@
                 (conv_value_in, conv_value),
                 (gain_in, gain),
                 (docs_in, docs),
+                (tokens.at[quarter, :], quarter_stage),
+                (tokens.at[pl.ds(128 - RIM, RIM), rim_lanes], rim_stage),
             ]
         )
     ]
@@ -226,9 +231,7 @@
             pltpu.make_async_copy(src, dst, y_sem.at[y]).start()
             pltpu.make_async_copy(piece, pieces.at[y], p_sem.at[y]).start()
 
-    quarter = pl.ds(pl.multiple_of(32 * x, 32), 32)
     lanes = [pl.ds(1024 * i, 1024) for i in range(2)]
-    rim_lanes = pl.ds(pl.multiple_of(512 * x, 512), 512)
 
     def tokens_out():
         owner = yl // 2 == c
@@ -237,14 +240,13 @@
             for j in range(1, 4):
                 to = 4 * group + lax.rem(yl + j, 4)
                 dst = x_all.at[rows, lanes[i]]
-                send(tokens.at[quarter, lanes[i]], dst, a1_sem.at[yl % 2, i], (to, head), owner)
+                send(quarter_stage.at[:, lanes[i]], dst, a1_sem.at[yl % 2, i], (to, head), owner)
         after_two = (c == 0) & (yl == 1)
         after_four = (c == 1) & (yl == 3)
         for j in range(4):
-            last = tokens.at[pl.ds(128 - RIM, RIM), rim_lanes]
             to = jnp.where(after_two, 4 * group + j, lax.rem(4 * group + 4 + j, 64))
             dst = x_all.at[pl.ds(0, RIM), rim_lanes]
-            send(last, dst, rim_sem.at[0], (to, 2 * x + 1 - c), after_two | after_four)
+            send(rim_stage, dst, rim_sem.at[0], (to, 2 * x + 1 - c), after_two | after_four)
 
     for copy in inputs[8:]:
         copy.wait()
@@ -314,7 +316,7 @@
             rows = pl.ds(pl.multiple_of(RIM + 128 * k + 32 * x, 16), 32)
             ref = x_all.at[rows, lanes[i]]
             pl.when(is_remote)(lambda ref=ref, k=k: arrived(ref, a1_sem.at[k, i]))
-            for j in (1, 3, 2):
+            for j in (2, 1, 3):
                 send(ref, ref, a2_sem.at[k, j - 1, i], (ctx, 2 * lax.rem(x + j, 4) + c), is_remote)
 
     def rim_on():
@@ -492,13 +494,16 @@
         rows = pl.ds(pl.multiple_of(256 * lax.rem(head + 8 - i, 8), 256), 256)
         arrived(wo_all.at[rows, :], wo_sem.at[i - 1])
     own_out.wait()
-    for i in range(8):
-        which = 2 * i + 1 - c
-        arrived(n_all.at[which], n_sem.at[which])
     total = jnp.zeros((128, 256), F32)
-    for i in range(8):
-        rows = jnp.concatenate([n_all[2 * i], n_all[2 * i + 1]], axis=1)
-        total = total + dot(rows, wo_all[256 * i : 256 * i + 256, :])
+    for core in (c, 1 - c):
+        for i in range(4):
+            pair = [4 * i + core, 4 * i + 2 + core]
+            for which in pair:
+                if core is not c:
+                    arrived(n_all.at[which], n_sem.at[which])
+            rows = jnp.concatenate([n_all[which] for which in pair], axis=1)
+            weights = [wo_all[pl.ds(pl.multiple_of(128 * which, 128), 128), :] for which in pair]
+            total = total + dot(rows, jnp.concatenate(weights, axis=0))
     out[...] = total.astype(BF16)
 
     for copy, cond in pending[done:]:
@@ -517,6 +522,8 @@
         in_specs=[pl.BlockSpec(memory_space=pltpu.HBM)] * 14,
         out_specs=vmem,
         scratch_shapes=[
+            pltpu.VMEM((32, 2048), BF16),
+            pltpu.VMEM((RIM, 512), BF16),
             pltpu.VMEM((2, 2, 32), BF16),
             pltpu.SMEM((2,), F32),
             pltpu.SMEM((2,), F32),
@@ -557,7 +564,7 @@
             dma,
             dma((16,)),
             dma((2,)),
-            dma((14,)),
+            dma((16,)),
         ],
         compiler_params=pltpu.CompilerParams(
             collective_id=0, has_side_effects=True, vmem_limit_bytes=60 * 2**20

time: 63 us -> 62.9 us (level)
  no operation moved by 1% of the time
where the time goes in v7:
time: 62.9 us; the launch traced here: 62.8 us
  Pallas kernels  62.1 us (99%)
  local copies, waits for them, and re-layouts  0.63 us (1%)
    pallas_call x1, Pallas kernels, local(): pl.pallas_call(kernel, out_shape=pltpu.VMEM((128, 256), BF16), in_specs=[...  62.1 us

profile of v7, /device:TPU:1, one launch (start us, length us, event | category | flops | bytes accessed | tf_op | source)
XLA Modules:
  0.0 62.8 jit_solution(10891758561572243698)
XLA Ops:
  0.0 62.1 %shard_map.136 = bf16[128,256]{1,0:T(8,128)(2,1)S(1)} custom-call(bf16[128,2048]{1,0:T(8,128)(2,1)} %tokens.1, bf16[32,128]{1,0:T(8,128)(2,1)} %w_query.1, bf16[32,128]{1,0:T(8,128)(2,1)} %w_key.1, bf16[32,256]{1,0:T(8,128)(2,1)} %w_value.1, bf16[32,256]{1,0:T(8,128)(2,1)} %w_gate.1, bf16[2,32]{1,0:T(2,128)(2,1)} %bitcast.3, bf16[2,32]{1,0:T(2,128)(2,1)} %bitcast.4, ...), custom_call_target="tpu_custom_call" | custom-call | tf_op jit(solution)/shard_map/pallas_call | solution.py:519
  62.1 0.6 %copy.16 = bf16[128,256]{1,0:T(8,128)(2,1)} copy(bf16[128,256]{1,0:T(8,128)(2,1)S(1)} %shard_map.136) | data formatting | bytes 131072
